TPU v7x, 32 devices: a whole 2x2x4 slice. The times are simulated.
32 devices in a mesh: dp: 8 (over z, x), seq: 4 (over y, core).
Axes of the slice: x: 2, y: 2, z: 4, core: 2. Of those that a mesh axis runs over, the one named last changes fastest.
Arguments:
- inputs: bfloat16 [4, 8, 512, 384], P(None, 'dp', 'seq'), may hold values from -6 to 6
- lengths: int32 [4, 8], P(None, 'dp'), may hold values from 1 to 512, as said below
- cotangent: bfloat16 [4, 8, 512, 384], P(None, 'dp', 'seq'), may hold values from -6 to 6
- pool_cotangent: bfloat16 [4, 8, 384], P(None, 'dp'), may hold values from -24 to 24
- qkv_weight: bfloat16 [384, 1152], replicated, may hold values from -0.4375 to 0.4375
- query_bias: float32 [384], replicated, may hold values from -3 to 3
- value_bias: float32 [384], replicated, may hold values from -3 to 3
- out_weight: bfloat16 [384, 384], replicated, may hold values from -1.75 to 1.75
- out_bias: float32 [384], replicated, may hold values from -3 to 3
- norm1_gain: float32 [384], replicated, may hold values from 0.5 to 1.5
- norm1_bias: float32 [384], replicated, may hold values from -2 to 2
- up_weight: bfloat16 [384, 1536], replicated, may hold values from -0.3125 to 0.3125
- up_bias: float32 [1536], replicated, may hold values from -3 to 3
- down_weight: bfloat16 [1536, 384], replicated, may hold values from -0.21875 to 0.21875
- down_bias: float32 [384], replicated, may hold values from -3 to 3
- norm2_gain: float32 [384], replicated, may hold values from 0.5 to 1.5
- norm2_bias: float32 [384], replicated, may hold values from -2 to 2
Outputs:
- block_out: bfloat16 [4, 8, 512, 384], P(None, 'dp', 'seq')
- pooled: float32 [4, 8, 384], P(None, 'dp')
- input_grad: bfloat16 [4, 8, 512, 384], P(None, 'dp', 'seq')
- grad_qkv_weight: float32 [384, 1152], replicated
- grad_query_bias: float32 [384], replicated
- grad_value_bias: float32 [384], replicated
- grad_out_weight: float32 [384, 384], replicated
- grad_out_bias: float32 [384], replicated
- grad_norm1_gain: float32 [384], replicated
- grad_norm1_bias: float32 [384], replicated
- grad_up_weight: float32 [384, 1536], replicated
- grad_up_bias: float32 [1536], replicated
- grad_down_weight: float32 [1536, 384], replicated
- grad_down_bias: float32 [384], replicated
- grad_norm2_gain: float32 [384], replicated
- grad_norm2_bias: float32 [384], replicated
Inputs may be any that keep to these rules, and one draw needn't show every extreme that they name: `lengths`: for every sequence index, at least one of the 4 micro-batches has length 512.
All inputs are finite; a program needn't handle non-finite values.
Results may differ from a plain program's by a relative error of at most 0.015.
The roundings to bfloat16 on the way count: a program that leaves them out, or rounds other values in their place, can miss the bound.
Values may be sent and summed in bfloat16 or wider, within the bound.
A program may use at most 128 MiB of HBM per device.

v0:
```python
import jax
import jax.numpy as jnp
from jax import lax
from jax.sharding import PartitionSpec as P

H = 12
HD = 32


epsilon = 1e-06
masked_value = -1e30


def norm_forward(values, scale_gain, shift):
    centre = values - jnp.mean(values, axis=-1, keepdims=True)
    inverse = lax.rsqrt(jnp.mean(centre * centre, axis=-1, keepdims=True) + epsilon)
    normal = centre * inverse
    return (normal * scale_gain + shift, normal, inverse)


def norm_backward(grad_out, normal, inverse, scale_gain):
    grad_gain = jnp.sum(grad_out * normal, axis=0)
    grad_shift = jnp.sum(grad_out, axis=0)
    scaled = grad_out * scale_gain
    grad_in = inverse * (
        scaled
        - jnp.mean(scaled, axis=-1, keepdims=True)
        - normal * jnp.mean(scaled * normal, axis=-1, keepdims=True)
    )
    return (grad_in, grad_gain, grad_shift)


def masked_scores(query, keys, valid):
    scores = jnp.einsum(
        "bqhd,bkhd->bhqk", query, keys, preferred_element_type=jnp.float32
    ) * query.shape[-1] ** (-0.5)
    return jnp.where(valid[:, None, None, :], scores, masked_value)


def attend_block(query, keys, values, valid):
    scores = masked_scores(query, keys, valid)
    peak = jnp.max(scores, axis=-1, keepdims=True)
    raised = jnp.exp(scores - peak)
    total = jnp.sum(raised, axis=-1, keepdims=True)
    weights = (raised / total).astype(jnp.bfloat16)
    context = jnp.einsum("bhqk,bkhd->bqhd", weights, values, preferred_element_type=jnp.float32)
    return (context, (peak + jnp.log(total))[..., 0])


def score_grads(query, keys, values, valid, logsum, grad_context, inner):
    scores = masked_scores(query, keys, valid)
    probs = jnp.exp(scores - logsum[..., None])
    grad_weights = jnp.einsum(
        "bqhd,bkhd->bhqk", grad_context, values, preferred_element_type=jnp.float32
    )
    inner = jnp.sum(probs * grad_weights, axis=-1)
    grad_scores = (probs * (grad_weights - inner[..., None])).astype(jnp.bfloat16)
    return (probs, grad_scores, inner)


def attend_back(query, keys, values, valid, logsum, grad_context):
    scale = query.shape[-1] ** (-0.5)
    probs, grad_scores, inner = score_grads(query, keys, values, valid, logsum, grad_context, None)
    grad_query = (
        jnp.einsum("bhqk,bkhd->bqhd", grad_scores, keys, preferred_element_type=jnp.float32) * scale
    )
    grad_keys = (
        jnp.einsum("bhqk,bqhd->bkhd", grad_scores, query, preferred_element_type=jnp.float32)
        * scale
    )
    grad_values = jnp.einsum(
        "bhqk,bqhd->bkhd",
        probs.astype(jnp.bfloat16),
        grad_context,
        preferred_element_type=jnp.float32,
    )
    return (grad_query, grad_keys, grad_values)


def group_size():
    group = 1
    return group


def blockwise(function, arrays, count):
    grouped = tuple(
        (item.reshape((item.shape[0] // count, count) + item.shape[1:]) for item in arrays)
    )
    results = lax.map(lambda items: function(*items), grouped)
    return tuple((item.reshape((-1,) + item.shape[2:]) for item in results))


def gelu_slope(upper):
    cdf_part = 0.5 * (1.0 + lax.erf(upper * 2.0 ** (-0.5)))
    density = jnp.exp(-0.5 * upper * upper) * (2.0 * jnp.pi) ** (-0.5)
    return cdf_part + upper * density


def body(
    inputs,
    lengths,
    cotangent,
    pool_cotangent,
    qkv_weight,
    query_bias,
    value_bias,
    out_weight,
    out_bias,
    norm1_gain,
    norm1_bias,
    up_weight,
    up_bias,
    down_weight,
    down_bias,
    norm2_gain,
    norm2_bias,
):
    micros, seqs, local, width = inputs.shape
    full_len = local * lax.axis_size("seq")
    offset = lax.axis_index("seq") * local
    group = group_size()
    positions = jnp.arange(full_len)
    bias_row = jnp.concatenate([query_bias, jnp.zeros_like(query_bias), value_bias])
    weights_all = (
        qkv_weight,
        query_bias,
        value_bias,
        out_weight,
        out_bias,
        norm1_gain,
        norm1_bias,
        up_weight,
        up_bias,
        down_weight,
        down_bias,
        norm2_gain,
        norm2_bias,
    )
    totals = tuple((jnp.zeros(item.shape, jnp.float32) for item in weights_all))
    block_list = []
    pooled_list = []
    input_list = []
    for micro in range(micros):
        rows_in = inputs[micro].reshape(-1, width)
        spans = lengths[micro]
        valid = positions[None, :] < spans[:, None]
        valid_here = lax.dynamic_slice_in_dim(valid, offset, local, 1)
        here = valid_here.reshape(-1, 1)
        projected = jnp.dot(rows_in, qkv_weight, preferred_element_type=jnp.float32) + bias_row
        joined = projected.astype(jnp.bfloat16)
        query = joined[:, :width].reshape(seqs, local, H, HD)
        keys_here = joined[:, width : 2 * width].reshape(seqs, local, width)
        values_here = joined[:, 2 * width :].reshape(seqs, local, width)
        keys_all, values_all = (
            lax.all_gather(keys_here, "seq", axis=1, tiled=True),
            lax.all_gather(values_here, "seq", axis=1, tiled=True),
        )
        keys_full = keys_all.reshape(seqs, full_len, H, HD)
        values_full = values_all.reshape(seqs, full_len, H, HD)
        context, logsum = blockwise(attend_block, (query, keys_full, values_full, valid), group)
        context_low = context.reshape(-1, width).astype(jnp.bfloat16)
        attended = jnp.dot(context_low, out_weight, preferred_element_type=jnp.float32) + out_bias
        first, first_normal, first_inverse = norm_forward(
            rows_in.astype(jnp.float32) + attended, norm1_gain, norm1_bias
        )
        first_low = first.astype(jnp.bfloat16)
        upper = jnp.dot(first_low, up_weight, preferred_element_type=jnp.float32) + up_bias
        active = jax.nn.gelu(upper, approximate=False).astype(jnp.bfloat16)
        lower = jnp.dot(active, down_weight, preferred_element_type=jnp.float32) + down_bias
        second, second_normal, second_inverse = norm_forward(first + lower, norm2_gain, norm2_bias)
        masked = jnp.where(here, second, 0.0)
        block_list.append(masked.reshape(seqs, local, width).astype(jnp.bfloat16))
        pooled_part = jnp.sum(masked.reshape(seqs, local, width), axis=1)
        counts = spans.astype(jnp.float32)
        pooled_list.append(lax.psum(pooled_part, "seq") / counts[:, None])
        pool_share = pool_cotangent[micro].astype(jnp.float32) / counts[:, None]
        grad_result = cotangent[micro].astype(jnp.float32) + pool_share[:, None, :]
        grad_result = jnp.where(here, grad_result.reshape(-1, width), 0.0)
        grad_sum2, grad_gain2, grad_shift2 = norm_backward(
            grad_result, second_normal, second_inverse, norm2_gain
        )
        grad_lower = grad_sum2.astype(jnp.bfloat16)
        grad_down = jnp.einsum("rf,rd->fd", active, grad_lower, preferred_element_type=jnp.float32)
        grad_down_b = jnp.sum(grad_lower.astype(jnp.float32), axis=0)
        grad_active = jnp.einsum(
            "rd,fd->rf", grad_lower, down_weight, preferred_element_type=jnp.float32
        )
        grad_upper = (grad_active * gelu_slope(upper)).astype(jnp.bfloat16)
        grad_up = jnp.einsum("rd,rf->df", first_low, grad_upper, preferred_element_type=jnp.float32)
        grad_up_b = jnp.sum(grad_upper.astype(jnp.float32), axis=0)
        grad_first = grad_sum2 + jnp.einsum(
            "rf,df->rd", grad_upper, up_weight, preferred_element_type=jnp.float32
        )
        grad_hidden, grad_gain1, grad_shift1 = norm_backward(
            grad_first, first_normal, first_inverse, norm1_gain
        )
        grad_attended = grad_hidden.astype(jnp.bfloat16)
        grad_out = jnp.einsum(
            "rc,rd->cd", context_low, grad_attended, preferred_element_type=jnp.float32
        )
        grad_out_b = jnp.sum(grad_attended.astype(jnp.float32), axis=0)
        grad_context = jnp.einsum(
            "rd,cd->rc", grad_attended, out_weight, preferred_element_type=jnp.float32
        )
        grad_context = grad_context.astype(jnp.bfloat16).reshape(seqs, local, H, HD)
        keys_back, values_back = (
            lax.all_gather(keys_here, "seq", axis=1, tiled=True),
            lax.all_gather(values_here, "seq", axis=1, tiled=True),
        )
        keys_use = keys_back.reshape(seqs, full_len, H, HD)
        values_use = values_back.reshape(seqs, full_len, H, HD)
        grad_query, grad_keys_all, grad_values_all = blockwise(
            attend_back, (query, keys_use, values_use, valid, logsum, grad_context), group
        )
        grad_keys, grad_values = (
            lax.psum_scatter(
                grad_keys_all.reshape(seqs, full_len, width).astype(jnp.bfloat16),
                "seq",
                scatter_dimension=1,
                tiled=True,
            ).astype(jnp.float32),
            lax.psum_scatter(
                grad_values_all.reshape(seqs, full_len, width).astype(jnp.bfloat16),
                "seq",
                scatter_dimension=1,
                tiled=True,
            ).astype(jnp.float32),
        )
        grad_joined = jnp.concatenate(
            [
                grad_query.reshape(-1, width),
                grad_keys.reshape(-1, width),
                grad_values.reshape(-1, width),
            ],
            axis=1,
        ).astype(jnp.bfloat16)
        grad_qkv = jnp.einsum("rd,re->de", rows_in, grad_joined, preferred_element_type=jnp.float32)
        grad_query_b = jnp.sum(grad_joined[:, :width].astype(jnp.float32), axis=0)
        grad_value_b = jnp.sum(grad_joined[:, 2 * width :].astype(jnp.float32), axis=0)
        grad_rows = grad_hidden + jnp.einsum(
            "re,de->rd", grad_joined, qkv_weight, preferred_element_type=jnp.float32
        )
        input_list.append(grad_rows.reshape(seqs, local, width).astype(jnp.bfloat16))
        terms = (
            grad_qkv,
            grad_query_b,
            grad_value_b,
            grad_out,
            grad_out_b,
            grad_gain1,
            grad_shift1,
            grad_up,
            grad_up_b,
            grad_down,
            grad_down_b,
            grad_gain2,
            grad_shift2,
        )
        totals = tuple((left + right for left, right in zip(totals, terms)))
    totals = lax.psum(totals, ("dp", "seq"))
    return (
        jnp.stack(block_list),
        jnp.stack(pooled_list),
        jnp.stack(input_list),
        totals[0],
        totals[1],
        totals[2],
        totals[3],
        totals[4],
        totals[5],
        totals[6],
        totals[7],
        totals[8],
        totals[9],
        totals[10],
        totals[11],
        totals[12],
    )


def solution(mesh):
    return jax.shard_map(
        body,
        mesh=mesh,
        in_specs=(
            P(None, "dp", "seq", None),
            P(None, "dp"),
            P(None, "dp", "seq", None),
            P(None, "dp", None),
            P(),
            P(),
            P(),
            P(),
            P(),
            P(),
            P(),
            P(),
            P(),
            P(),
            P(),
            P(),
            P(),
        ),
        out_specs=(
            P(None, "dp", "seq", None),
            P(None, "dp", None),
            P(None, "dp", "seq", None),
            P(),
            P(),
            P(),
            P(),
            P(),
            P(),
            P(),
            P(),
            P(),
            P(),
            P(),
            P(),
            P(),
        ),
        check_vma=False,
    )
```

profile of v0, /device:TPU:0, one launch (start us, length us, event | category | flops | bytes accessed | tf_op | source)
XLA Modules:
  0.0 527.7 jit_solution(14383355308078743938)
XLA Ops:
  9.7 2.3 fusion.10
  25.9 7.9 %all-gather = bf16[512,384]{1,0:T(8,128)(2,1)S(1)} all-gather(bf16[128,384]{1,0:T(8,128)(2,1)S(1)} %get-tuple-element.355), channel_id=2, replica_groups=mesh['dp'=8,'seq'=4] {'seq'}, dimensions={0}, use_global_device_ids=true | all-gather | bytes 491520 | tf_op jit(solution)/shard_map/all_gather | solution.py:156
  34.2 6.6 %all-gather.1 = bf16[512,384]{1,0:T(8,128)(2,1)S(1)} all-gather(bf16[128,384]{1,0:T(8,128)(2,1)S(1)} %get-tuple-element.353), channel_id=3, replica_groups=mesh['dp'=8,'seq'=4] {'seq'}, dimensions={0}, use_global_device_ids=true | all-gather | bytes 491520 | tf_op jit(solution)/shard_map/all_gather | solution.py:155
  45.1 6.6 %all-gather.2 = bf16[512,384]{1,0:T(8,128)(2,1)S(1)} all-gather(bf16[128,384]{1,0:T(8,128)(2,1)S(1)} %get-tuple-element.358), channel_id=4, replica_groups=mesh['dp'=8,'seq'=4] {'seq'}, dimensions={0}, use_global_device_ids=true | all-gather | bytes 491520 | tf_op jit(solution)/shard_map/all_gather | solution.py:156
  52.0 6.9 %all-gather.3 = bf16[512,384]{1,0:T(8,128)(2,1)S(1)} all-gather(bf16[128,384]{1,0:T(8,128)(2,1)S(1)} %get-tuple-element.356), channel_id=5, replica_groups=mesh['dp'=8,'seq'=4] {'seq'}, dimensions={0}, use_global_device_ids=true | all-gather | bytes 491520 | tf_op jit(solution)/shard_map/all_gather | solution.py:155
  62.7 2.8 fusion.75
  65.5 2.8 fusion.78
  72.3 6.6 %all-gather.6 = bf16[512,384]{1,0:T(8,128)(2,1)S(1)} all-gather(bf16[128,384]{1,0:T(8,128)(2,1)S(1)} %get-tuple-element.364), channel_id=8, replica_groups=mesh['dp'=8,'seq'=4] {'seq'}, dimensions={0}, use_global_device_ids=true | all-gather | bytes 491520 | tf_op jit(solution)/shard_map/all_gather | solution.py:156
  81.4 8.7 %all-gather.7 = bf16[512,384]{1,0:T(8,128)(2,1)} all-gather(bf16[128,384]{1,0:T(8,128)(2,1)} %get-tuple-element.362), channel_id=9, replica_groups=mesh['dp'=8,'seq'=4] {'seq'}, dimensions={0}, use_global_device_ids=true | all-gather | bytes 491520 | tf_op jit(solution)/shard_map/all_gather | solution.py:155
  96.8 2.8 fusion.84
  102.6 7.0 %all-gather.4 = bf16[512,384]{1,0:T(8,128)(2,1)} all-gather(bf16[128,384]{1,0:T(8,128)(2,1)S(1)} %get-tuple-element.361), channel_id=6, replica_groups=mesh['dp'=8,'seq'=4] {'seq'}, dimensions={0}, use_global_device_ids=true | all-gather | bytes 491520 | tf_op jit(solution)/shard_map/all_gather | solution.py:156
  111.7 8.0 %all-gather.5 = bf16[512,384]{1,0:T(8,128)(2,1)} all-gather(bf16[128,384]{1,0:T(8,128)(2,1)} %get-tuple-element.359), channel_id=7, replica_groups=mesh['dp'=8,'seq'=4] {'seq'}, dimensions={0}, use_global_device_ids=true | all-gather | bytes 491520 | tf_op jit(solution)/shard_map/all_gather | solution.py:155
  145.8 3.6 fusion.46
  149.3 2.9 copy.114
  159.7 2.9 copy.112
  168.8 2.4 fusion.43
  171.2 2.9 copy.110
  181.3 2.9 copy.108
  190.4 2.4 fusion.40
  192.8 2.9 copy.106
  202.9 3.0 copy.104
  210.5 2.4 fusion.37
  213.0 2.9 copy.102
  226.3 2.4 fusion.64
  228.8 2.3 fusion.63
  240.1 8.2 %all-reduce.2 = (f32[1,384]{1,0:T(1,128)}, f32[1,384]{1,0:T(1,128)}, f32[1,384]{1,0:T(1,128)}, f32[1,384]{1,0:T(1,128)}) all-reduce(f32[1,384]{1,0:T(1,128)} %reduce_sum.763, f32[1,384]{1,0:T(1,128)} %reduce_sum.761, f32[1,384]{1,0:T(1,128)} %reduce_sum.759, f32[1,384]{1,0:T(1,128)} %reduce_sum.757), channel_id=1, replica_groups=mesh['dp'=8,'seq'=4] {'seq'}, use_global_device_ids=true, to_apply=%region_31.32 | all-reduce | flops 1536 | bytes 12288 | tf_op jit(solution)/shard_map/psum | solution.py:175
  272.6 21.3 %reduce-scatter.29.cloned.1.call-done = bf16[128,384]{1,0:T(8,128)(2,1)} async-done(((bf16[512,384]{1,0:T(8,128)(2,1)}), bf16[128,384]{1,0:T(8,128)(2,1)}) %reduce-scatter.29.cloned.1.call-update) | async-done | bytes 98320
  295.1 22.2 %reduce-scatter.27.cloned.1.call-done = bf16[128,384]{1,0:T(8,128)(2,1)} async-done(((bf16[512,384]{1,0:T(8,128)(2,1)}), bf16[128,384]{1,0:T(8,128)(2,1)}) %reduce-scatter.27.cloned.1.call-update) | async-done | bytes 98320
  318.5 22.2 %reduce-scatter.25.cloned.1.call-done = bf16[128,384]{1,0:T(8,128)(2,1)} async-done(((bf16[512,384]{1,0:T(8,128)(2,1)}), bf16[128,384]{1,0:T(8,128)(2,1)}) %reduce-scatter.25.cloned.1.call-update) | async-done | bytes 98320
  347.5 41.7 %all-reduce = (f32[384]{0:T(512)}, f32[384]{0:T(512)}, f32[384]{0:T(512)}, f32[384]{0:T(512)}, f32[384]{0:T(512)}, /*index=5*/f32[1536]{0:T(1024)}, f32[384]{0:T(512)}, f32[384]{0:T(512)}, f32[384]{0:T(512)}) all-reduce(f32[384]{0:T(512)S(1)} %add_add_fusion.8, ...), channel_id=1, replica_groups=mesh['dp'=8,'seq'=4] {'dp','seq'}, use_global_device_ids=true, to_apply=%region_65.66 | all-reduce | flops 4608 | bytes 36864 | tf_op jit(solution)/shard_map/psum | solution.py:260
  391.7 122.4 %all-reduce.5.cloned.1.call-done = (f32[384,1152]{0,1:T(8,128)}, f32[384,384]{1,0:T(8,128)}, f32[384,1536]{1,0:T(8,128)}, f32[1536,384]{1,0:T(8,128)}) async-done(((f32[384,1152]{0,1:T(8,128)}, f32[384,384]{1,0:T(8,128)}, f32[384,1536]{1,0:T(8,128)}, f32[1536,384]{1,0:T(8,128)}), (f32[384,1152]{0,1:T(8,128)}, f32[384,384]{1,0:T(8,128)}, f32[384,1536]{1,0:T(8,128)}, ...) | async-done | bytes 7077904 | tf_op jit(solution)/shard_map/psum | solution.py:260
  514.2 2.9 copy.99
  (647 shorter events, 161.9 us)
Async XLA Ops:
  7.2 55.5 %copy-start = (bf16[384,1536]{1,0:T(8,128)(2,1)S(1)}, bf16[384,1536]{1,0:T(8,128)(2,1)}, u32[]{:S(2)}) copy-start(bf16[384,1536]{1,0:T(8,128)(2,1)} %param.28) | copy-start | bytes 3538948
  7.2 259.4 %reduce-scatter.39.cloned.1.call-start = ((), (), s32[]{:S(2)}) async-start(), calls=%async_computation.15 | async-start | bytes 491520
  44.3 96.9 %copy-start.29 = (f32[128,384]{1,0:T(8,128)}, f32[128,384]{1,0:T(8,128)S(1)}, u32[]{:S(2)}) copy-start(f32[128,384]{1,0:T(8,128)S(1)} %get-tuple-element.392) | copy-start | bytes 589828
  44.3 24.0 %copy-start.128 = (f32[128]{0:T(128)}, f32[128]{0:T(128)S(1)}, u32[]{:S(2)}) copy-start(f32[128]{0:T(128)S(1)} %broadcast_multiply_fusion.23) | copy-start | bytes 1540
  51.9 8.9 %copy-start.64 = (bf16[512,384]{0,1:T(8,128)(2,1)}, bf16[512,384]{0,1:T(8,128)(2,1)S(1)}, u32[]{:S(2)}) copy-start(bf16[512,384]{0,1:T(8,128)(2,1)S(1)} %copy.86) | copy-start | bytes 1179652
  62.4 80.7 %copy-start.23 = (f32[128,384]{1,0:T(8,128)}, f32[128,384]{1,0:T(8,128)S(1)}, u32[]{:S(2)}) copy-start(f32[128,384]{1,0:T(8,128)S(1)} %get-tuple-element.400) | copy-start | bytes 589828
  69.4 21.9 %copy-start.203 = (pred[512]{0:T(512)(128)(4,1)S(1)}, pred[512]{0:T(512)(128)(4,1)}, u32[]{:S(2)}) copy-start(pred[512]{0:T(512)(128)(4,1)} %iota_compare_fusion) | copy-start | bytes 1540
  96.5 46.6 %copy-start.25 = (f32[128,384]{1,0:T(8,128)}, f32[128,384]{1,0:T(8,128)S(1)}, u32[]{:S(2)}) copy-start(f32[128,384]{1,0:T(8,128)S(1)} %get-tuple-element.416) | copy-start | bytes 589828
  111.7 12.6 %copy-start.93 = (bf16[128,384]{0,1:T(8,128)(2,1)}, bf16[128,384]{0,1:T(8,128)(2,1)S(1)}, u32[]{:S(2)}) copy-start(bf16[128,384]{0,1:T(8,128)(2,1)S(1)} %copy.90) | copy-start | bytes 294916
  126.9 16.2 %copy-start.27 = (f32[128,384]{1,0:T(8,128)}, f32[128,384]{1,0:T(8,128)S(1)}, u32[]{:S(2)}) copy-start(f32[128,384]{1,0:T(8,128)S(1)} %get-tuple-element.408) | copy-start | bytes 589828
  126.9 16.2 %copy-start.131 = (f32[128]{0:T(128)}, f32[128]{0:T(128)S(1)}, u32[]{:S(2)}) copy-start(f32[128]{0:T(128)S(1)} %broadcast_multiply_fusion.19) | copy-start | bytes 1540
  127.1 16.0 %copy-start.196 = (f32[128]{0:T(128)}, f32[128]{0:T(128)S(1)}, u32[]{:S(2)}) copy-start(f32[128]{0:T(128)S(1)} %add_rsqrt_fusion.3) | copy-start | bytes 1540
  154.3 113.6 %reduce-scatter.37.cloned.1.call-start = ((), (), s32[]{:S(2)}) async-start(), calls=%async_computation.14 | async-start | bytes 491520
  158.6 10.2 %copy-start.7 = (f32[12,128,512]{2,1,0:T(8,128)S(1)}, f32[12,128,512]{2,1,0:T(8,128)}, u32[]{:S(2)}) copy-start(f32[12,128,512]{2,1,0:T(8,128)} %copy-done.6) | copy-start | bytes 9437188
  164.6 104.5 %reduce-scatter.35.cloned.1.call-start = ((), (), s32[]{:S(2)}) async-start(), calls=%async_computation.13 | async-start | bytes 491520
  176.1 94.2 %reduce-scatter.33.cloned.1.call-start = ((), (), s32[]{:S(2)}) async-start(), calls=%async_computation.12 | async-start | bytes 491520
  180.2 10.2 %copy-start.5 = (f32[12,128,512]{2,1,0:T(8,128)S(1)}, f32[12,128,512]{2,1,0:T(8,128)}, u32[]{:S(2)}) copy-start(f32[12,128,512]{2,1,0:T(8,128)} %copy-done.4) | copy-start | bytes 9437188
  186.2 85.3 %reduce-scatter.31.cloned.1.call-start = ((), (), s32[]{:S(2)}) async-start(), calls=%async_computation.11 | async-start | bytes 491520
  197.7 96.2 %reduce-scatter.29.cloned.1.call-start = ((), (), s32[]{:S(2)}) async-start(), calls=%async_computation.10 | async-start | bytes 491520
  207.8 109.5 %reduce-scatter.27.cloned.1.call-start = ((), (), s32[]{:S(2)}) async-start(), calls=%async_computation.9 | async-start | bytes 491520
  217.9 122.8 %reduce-scatter.25.cloned.1.call-start = ((), (), s32[]{:S(2)}) async-start(), calls=%async_computation.8 | async-start | bytes 491520
  226.0 288.2 %all-reduce.5.cloned.1.call-start = ((), (), s32[]{:S(2)}) async-start(), calls=%async_computation.16 | async-start | bytes 14155776 | tf_op jit(solution)/shard_map/psum | solution.py:260
  234.1 19.3 %copy-start.52 = (f32[128,384]{1,0:T(8,128)S(1)}, f32[128,384]{1,0:T(8,128)}, u32[]{:S(2)}) copy-start(f32[128,384]{1,0:T(8,128)} %get-tuple-element.342) | copy-start | bytes 589828
  234.7 19.8 %copy-start.53 = (f32[128,384]{1,0:T(8,128)S(1)}, f32[128,384]{1,0:T(8,128)}, u32[]{:S(2)}) copy-start(f32[128,384]{1,0:T(8,128)} %get-tuple-element.384) | copy-start | bytes 589828
  236.8 21.0 %copy-start.24 = (f32[128,384]{1,0:T(8,128)S(1)}, f32[128,384]{1,0:T(8,128)}, u32[]{:S(2)}) copy-start(f32[128,384]{1,0:T(8,128)} %copy-done.23) | copy-start | bytes 589828
  236.8 21.0 %copy-start.124 = (f32[128]{0:T(128)S(1)}, f32[128]{0:T(128)}, u32[]{:S(2)}) copy-start(f32[128]{0:T(128)} %copy-done.122) | copy-start | bytes 1540
  236.8 21.0 %copy-start.189 = (f32[128]{0:T(128)S(1)}, f32[128]{0:T(128)}, u32[]{:S(2)}) copy-start(f32[128]{0:T(128)} %copy-done.187) | copy-start | bytes 1540
  248.3 9.5 %copy-start.69 = (bf16[128,1536]{1,0:T(8,128)(2,1)S(1)}, bf16[128,1536]{1,0:T(8,128)(2,1)}, u32[]{:S(2)}) copy-start(bf16[128,1536]{1,0:T(8,128)(2,1)} %copy-done.68) | copy-start | bytes 1179652
  266.1 75.7 %copy-start.40 = (bf16[4,1,128,384]{3,2,1,0:T(8,128)(2,1)S(1)}, bf16[4,1,128,384]{3,2,1,0:T(8,128)(2,1)}, u32[]{:S(2)}) copy-start(bf16[4,1,128,384]{3,2,1,0:T(8,128)(2,1)} %param.17) | copy-start | bytes 1179652
  344.9 44.4 %copy-start.13 = (bf16[384,1152]{1,0:T(8,128)(2,1)S(1)}, bf16[384,1152]{1,0:T(8,128)(2,1)}, u32[]{:S(2)}) copy-start(bf16[384,1152]{1,0:T(8,128)(2,1)} %param.21) | copy-start | bytes 2654212
  344.9 44.3 %copy-start.55 = (f32[128,384]{1,0:T(8,128)S(1)}, f32[128,384]{1,0:T(8,128)}, u32[]{:S(2)}) copy-start(f32[128,384]{1,0:T(8,128)} %copy-done.54) | copy-start | bytes 589828
  345.3 45.2 %copy-start.51 = (f32[128,384]{1,0:T(8,128)S(1)}, f32[128,384]{1,0:T(8,128)}, u32[]{:S(2)}) copy-start(f32[128,384]{1,0:T(8,128)} %get-tuple-element.344) | copy-start | bytes 589828
  (187 other events, 536.8 us)
Sparse Core Ops, SparseCore 0:
  154.4 21.7 reduce-scatter.38
  179.3 20.8 reduce-scatter.36
  202.7 20.8 reduce-scatter.34
  226.5 20.9 reduce-scatter.32
  249.8 20.8 reduce-scatter.30
  273.1 20.8 reduce-scatter.28
  296.4 20.8 reduce-scatter.26
  319.8 20.8 reduce-scatter.24
  348.1 166.0 all-reduce.4
where the time goes:
time: 534 us; the launch traced here: 528 us
  waiting for transfers between devices  188 us (35%)
  blocking collectives  108 us (20%)
  matrix products  94.8 us (18%)
  local copies, waits for them, and re-layouts  80.4 us (15%)
  other arithmetic  35.3 us (7%)
  between operations  19.9 us (4%)
    psum x1, waiting for transfers between devices, body(): totals = lax.psum(totals, ('dp', 'seq'))  122 us
    unnamed x17, waiting for transfers between devices  65.9 us
    unnamed x456, local copies, waits for them, and re-layouts  62.7 us
    psum x1, blocking collectives, body(): totals = lax.psum(totals, ('dp', 'seq'))  41.7 us
    all_gather x4, blocking collectives, body(): lax.all_gather(keys_here, 'seq', axis=1, tiled=True)  30.2 us
    all_gather x4, blocking collectives, body(): lax.all_gather(values_here, 'seq', axis=1, tiled=True)  28.1 us
    dot_general x4, matrix products, attend_back(): jnp.einsum('bhqk,bqhd->bkhd', probs.astype(jnp.bfloat16), grad_context, p...  10.7 us
  transfers between devices with their start and end apart: 9, of which 4 were waited for; matrix products, arithmetic and copies ran while one was open for 20% of the time, Pallas kernels for 0%

commit v1 on v0

v1 whole, which is shorter than its diff:
```python
import functools

import jax
import jax.numpy as jnp
from jax import lax
from jax.experimental import pallas as pl
from jax.experimental.pallas import tpu as pltpu
from jax.sharding import PartitionSpec as P

H = 12
HD = 32
D = 384
FF = 1536
EPS = 1e-6
F32 = jnp.float32
BF16 = jnp.bfloat16
MESH = pl.DeviceIdType.MESH
NN = (((1,), (0,)), ((), ()))
NT = (((1,), (1,)), ((), ()))
TN = (((0,), (0,)), ((), ()))
LOG2E = 1.4426950408889634
SCALE = HD**-0.5
VROWS = HD + 16
CHUNKS = 3
ROWS = 1536


def dot(left, right, dims):
    return lax.dot_general(left, right, dims, preferred_element_type=F32)


def gelu_and_slope(upper):
    cdf = 0.5 * (1.0 + lax.erf(upper * 2.0**-0.5))
    density = jnp.exp2((-0.5 * LOG2E) * (upper * upper)) * (2.0 * jnp.pi) ** -0.5
    return upper * cdf, cdf + upper * density


def layer_norm(values):
    centre = values - jnp.mean(values, axis=-1, keepdims=True)
    inverse = lax.rsqrt(jnp.mean(centre * centre, axis=-1, keepdims=True) + EPS)
    return centre * inverse, inverse


def norm_back(grad_out, normal, inverse, gain):
    scaled = grad_out * gain
    return inverse * (
        scaled
        - jnp.mean(scaled, axis=-1, keepdims=True)
        - normal * jnp.mean(scaled * normal, axis=-1, keepdims=True)
    )


def kernel(
    ndp,
    inputs_ref, lengths_ref, cot_ref, pool_ref,
    qkv_hbm, qb_ref, vb_ref, out_hbm, ob_ref, g1_ref, b1_ref,
    up_hbm, ub_ref, down_hbm, db_ref, g2_ref, b2_ref,
    block_ref, pooled_ref, igrad_ref, grads_ref, small_ref,
    x, cot, qkv_w, out_w, up_w, down_w, qkv_t, x_t,
    q_t, kd_t, kz_t, v_x, probs, inv, c_t, y1, r1, first_low, active, slope,
    lower, gsum, g_low, g_up, g_hid, gc_t, gj_t, bout, igr, pool,
    part, got0, got1, got2, got3, shard1, shard2, shard3, full, small, small_got,
    w_sem, loc_sem, in_send, in_recv, out_send, out_recv, pool_send, pool_recv,
    rs_send, rs_recv, ag_send, ag_recv, sm_send, sm_recv, fin_sem,
):
    dp = lax.axis_index("dp")
    sq = lax.axis_index("seq")
    core = lax.rem(sq, 2)
    yy = lax.div(sq, 2)
    xx = lax.rem(dp, 2)
    zz = lax.rem(lax.div(dp, 2), 4)
    extra = []
    bit = 8
    while bit < ndp:
        extra.append(bit)
        bit *= 2

    def flip(index, amount):
        digit = lax.rem(lax.div(index, amount), 2)
        return index + amount * (1 - 2 * digit)

    seq_peers = [lax.rem(sq + step, 4) for step in (1, 2, 3)]
    core_peer = (dp, flip(sq, 1))
    y_peer = (dp, flip(sq, 2))
    x_peer = (flip(dp, 1), sq)
    z_ids = [lax.rem(zz + step, 4) for step in (1, 2, 3)]
    z_peers = [(dp + 2 * (other - zz), sq) for other in z_ids]
    w_peers = [(flip(dp, amount), sq) for amount in extra]
    greeted = [(dp, peer) for peer in seq_peers] + [x_peer] + z_peers + w_peers

    loads = [
        pltpu.make_async_copy(src, dst, w_sem.at[i])
        for i, (src, dst) in enumerate(
            [(qkv_hbm, qkv_w), (out_hbm, out_w), (up_hbm, up_w), (down_hbm, down_w)]
        )
    ]
    for load in loads:
        load.start()
    own_rows = pl.ds(pl.multiple_of(sq * 128, 128), 128)
    own_x = pltpu.make_async_copy(inputs_ref.at[sq, 0], x.at[own_rows], loc_sem.at[0])
    own_c = pltpu.make_async_copy(cot_ref.at[sq, 0], cot.at[own_rows], loc_sem.at[1])
    own_x.start()
    own_c.start()

    barrier = pltpu.get_barrier_semaphore()
    for peer in greeted:
        pl.semaphore_signal(barrier, inc=1, device_id=peer, device_id_type=MESH)
    pl.semaphore_wait(barrier, len(greeted))

    def remote(src, dst, send, recv, peer):
        return pltpu.make_async_remote_copy(
            src_ref=src, dst_ref=dst, send_sem=send, recv_sem=recv,
            device_id=peer, device_id_type=MESH,
        )

    x_moves, c_moves = [], []
    for which, (src, dst, moves) in enumerate(((inputs_ref, x, x_moves), (cot_ref, cot, c_moves))):
        for i, peer in enumerate(seq_peers):
            move = remote(
                src.at[peer, 0], dst.at[own_rows],
                in_send.at[which, i], in_recv.at[which, i], (dp, peer),
            )
            move.start()
            moves.append(move)

    span = lengths_ref[sq, 0]
    count = span.astype(F32)
    lane_valid = lax.broadcasted_iota(jnp.int32, (1, 512), 1) < span

    loads[0].wait()

    def turn(i, carry):
        cols = pl.ds(pl.multiple_of(i * 128, 128), 128)
        qkv_t[cols, :] = qkv_w[:, cols].T
        return carry

    lax.fori_loop(0, 9, turn, 0)
    own_x.wait()
    for move in x_moves:
        move.wait()

    x_t[:D, :] = x[...].T
    x_t[D:, :] = jnp.ones((16, 512), BF16)

    qcol = jnp.broadcast_to(qb_ref[...], (8, D)).T[:, :1]
    vcol = jnp.broadcast_to(vb_ref[...], (8, D)).T[:, :1]
    q_t[...] = (dot(qkv_t[:D, :], x[...], NT) + qcol).astype(BF16)
    keys = dot(qkv_t[D : 2 * D, :], x[...], NT)
    kd_t[...] = jnp.where(lane_valid, keys, keys[:, :1]).astype(BF16)
    kz_t[...] = jnp.where(lane_valid, keys, 0.0).astype(BF16)
    values = jnp.where(lane_valid, dot(qkv_t[2 * D :, :], x[...], NT) + vcol, 0.0).astype(BF16)
    ones_row = jnp.broadcast_to(jnp.where(lane_valid, 1.0, 0.0), (16, 512)).astype(BF16)
    for h in range(H):
        v_x[h * VROWS : h * VROWS + HD, :] = values[h * HD : (h + 1) * HD, :]
        v_x[h * VROWS + HD : (h + 1) * VROWS, :] = ones_row

    def attend(h, carry):
        rows = pl.ds(pl.multiple_of(h * HD, HD), HD)
        scores = dot(kd_t[rows, :], q_t[rows, :], TN)
        peak = jnp.max(scores, axis=0, keepdims=True)
        raised = jnp.exp2(scores * (SCALE * LOG2E) - peak * (SCALE * LOG2E)).astype(BF16)
        probs[h] = raised
        both = dot(v_x[pl.ds(pl.multiple_of(h * VROWS, 16), VROWS), :], raised, NN)
        inverse = 1.0 / both[HD : HD + 1, :]
        inv[h] = jnp.broadcast_to(inverse, (8, 512))
        c_t[rows, :] = (both[:HD, :] * inverse).astype(BF16)
        return carry

    lax.fori_loop(0, H, attend, 0)

    loads[1].wait()

    def rows_of(i, size):
        return pl.ds(pl.multiple_of(i * size, size), size)

    lower[...] = dot(c_t[...], out_w[...], TN)

    def norm_one(i, carry):
        rows = rows_of(i, 128)
        normal, inverse = layer_norm(x[rows, :].astype(F32) + lower[rows, :] + ob_ref[...])
        y1[rows, :] = normal
        r1[rows, :] = inverse
        first_low[rows, :] = (normal * g1_ref[...] + b1_ref[...]).astype(BF16)
        return carry

    lax.fori_loop(0, 4, norm_one, 0)
    loads[2].wait()

    def raise_up(i, carry):
        cols = rows_of(i, 256)
        upper = dot(first_low[...], up_w[:, cols], NN) + ub_ref[:, cols]
        act, slp = gelu_and_slope(upper)
        active[:, cols] = act.astype(BF16)
        slope[:, cols] = slp
        return carry

    lax.fori_loop(0, FF // 256, raise_up, 0)
    loads[3].wait()
    lower[...] = dot(active[...], down_w[...], NN)
    own_c.wait()
    for move in c_moves:
        move.wait()
    pool_share = pool_ref[sq].astype(F32) / count

    zero_row = jnp.zeros((1, D), F32)

    def norm_two(i, carry):
        sums, gain_sum, bias_sum, down_sum = carry
        rows = rows_of(i, 128)
        firsts = y1[rows, :] * g1_ref[...] + b1_ref[...]
        normal, inverse = layer_norm(firsts + lower[rows, :] + db_ref[...])
        here = lax.broadcasted_iota(jnp.int32, (128, 1), 0) + i * 128 < span
        masked = jnp.where(here, normal * g2_ref[...] + b2_ref[...], 0.0)
        bout[rows, :] = masked.astype(BF16)
        grad = jnp.where(here, cot[rows, :].astype(F32) + pool_share, 0.0)
        grad_in = norm_back(grad, normal, inverse, g2_ref[...])
        gsum[rows, :] = grad_in
        low = grad_in.astype(BF16)
        g_low[rows, :] = low
        return (
            sums + jnp.sum(masked, axis=0, keepdims=True),
            gain_sum + jnp.sum(grad * normal, axis=0, keepdims=True),
            bias_sum + jnp.sum(grad, axis=0, keepdims=True),
            down_sum + jnp.sum(low.astype(F32), axis=0, keepdims=True),
        )

    sums, gain2, bias2, down_sum = lax.fori_loop(
        0, 4, norm_two, (zero_row, zero_row, zero_row, zero_row)
    )
    pool[sq] = jnp.broadcast_to(sums / count, (8, D))
    small[4:5, :] = down_sum
    small[10:11, :] = gain2
    small[11:12, :] = bias2

    out_moves = []
    for i, peer in enumerate(seq_peers):
        move = remote(
            bout.at[pl.ds(pl.multiple_of(peer * 128, 128), 128)], block_ref.at[sq, 0],
            out_send.at[0, i], out_recv.at[0, i], (dp, peer),
        )
        move.start()
        out_moves.append(move)
        move = remote(pool.at[sq], pool.at[sq], pool_send.at[i], pool_recv.at[i], (dp, peer))
        move.start()
        out_moves.append(move)
    own_b = pltpu.make_async_copy(bout.at[own_rows], block_ref.at[sq, 0], loc_sem.at[2])
    own_b.start()

    part[0] = dot(active[...], g_low[...], TN).astype(BF16)

    def back_up(i, carry):
        cols = rows_of(i, 256)
        low = (dot(g_low[...], down_w[cols, :], NT) * slope[:, cols]).astype(BF16)
        g_up[:, cols] = low
        return carry

    lax.fori_loop(0, FF // 256, back_up, 0)
    for i in range(4):
        small[i : i + 1, :] = jnp.sum(
            g_up[:, i * D : (i + 1) * D].astype(F32), axis=0, keepdims=True
        )
        part[1, i * D : (i + 1) * D, :] = dot(
            first_low[...], g_up[:, i * D : (i + 1) * D], TN
        ).astype(BF16)
    lower[...] = dot(g_up[...], up_w[...], NT)

    def norm_one_back(i, carry):
        gain_sum, bias_sum, out_sum = carry
        rows = rows_of(i, 128)
        grad = gsum[rows, :] + lower[rows, :]
        normal = y1[rows, :]
        grad_in = norm_back(grad, normal, r1[rows, :], g1_ref[...])
        g_hid[rows, :] = grad_in
        low = grad_in.astype(BF16)
        g_low[rows, :] = low
        return (
            gain_sum + jnp.sum(grad * normal, axis=0, keepdims=True),
            bias_sum + jnp.sum(grad, axis=0, keepdims=True),
            out_sum + jnp.sum(low.astype(F32), axis=0, keepdims=True),
        )

    gain1, bias1, out_sum = lax.fori_loop(0, 4, norm_one_back, (zero_row, zero_row, zero_row))
    small[5:6, :] = out_sum
    small[8:9, :] = gain1
    small[9:10, :] = bias1
    small[12:16, :] = jnp.zeros((4, D), F32)

    part[2, :D, :] = dot(c_t[...], g_low[...], NN).astype(BF16)
    gc_t[...] = dot(out_w[...], g_low[...], NT).astype(BF16)

    def attend_back(h, carry):
        rows = pl.ds(pl.multiple_of(h * HD, HD), HD)
        inverse = inv[h][:1, :]
        grad_c = (gc_t[rows, :].astype(F32) * inverse).astype(BF16)
        inner = jnp.sum(grad_c.astype(F32) * c_t[rows, :].astype(F32), axis=0, keepdims=True)
        grad_w = dot(v_x[pl.ds(pl.multiple_of(h * VROWS, 16), HD), :], grad_c, TN)
        weights = probs[h]
        grad_s = (weights.astype(F32) * (grad_w - inner)).astype(BF16)
        gj_t[rows, :] = (dot(kz_t[rows, :], grad_s, NN) * SCALE).astype(BF16)
        gk = jnp.where(lane_valid, dot(q_t[rows, :], grad_s, NT) * SCALE, 0.0)
        gj_t[pl.ds(pl.multiple_of(D + h * HD, HD), HD), :] = gk.astype(BF16)
        gv = jnp.where(lane_valid, dot(grad_c, weights, NT), 0.0)
        gj_t[pl.ds(pl.multiple_of(2 * D + h * HD, HD), HD), :] = gv.astype(BF16)
        return carry

    lax.fori_loop(0, H, attend_back, 0)

    for j in range(3):
        both = dot(x_t[...], gj_t[j * D : (j + 1) * D, :], NT)
        part[2, (j + 1) * D : (j + 2) * D, :] = both[:D, :].astype(BF16)
        if j == 0:
            small[6:7, :] = both[D : D + 1, :]
        if j == 2:
            small[7:8, :] = both[D : D + 1, :]
    igr[...] = (g_hid[...] + dot(gj_t[...], qkv_t[...], TN)).astype(BF16)
    for i, peer in enumerate(seq_peers):
        move = remote(
            igr.at[pl.ds(pl.multiple_of(peer * 128, 128), 128)], igrad_ref.at[sq, 0],
            out_send.at[1, i], out_recv.at[1, i], (dp, peer),
        )
        move.start()
        out_moves.append(move)
    own_i = pltpu.make_async_copy(igr.at[own_rows], igrad_ref.at[sq, 0], loc_sem.at[3])
    own_i.start()

    items = [(chunk, colour) for chunk in range(CHUNKS) for colour in range(3)]

    def lanes(colour):
        return pl.ds(colour * 128, 128)

    def piece(base, size):
        return pl.ds(pl.multiple_of(base, 16), size)

    half, quarter, eighth, unit = ROWS // 2, ROWS // 4, ROWS // 8, ROWS // 32

    def orders(colour):
        if colour == 0:
            return (yy, y_peer), (xx, x_peer)
        return (xx, x_peer), (yy, y_peer)

    def small_step(step, peer):
        move = remote(small, small_got.at[step], sm_send.at[step], sm_recv.at[step], peer)
        move.start()
        move.wait()
        small[...] = small[...] + small_got[step]

    moves = []
    for n, (chunk, colour) in enumerate(items):
        move = remote(
            part.at[chunk, piece((1 - core) * half, half), lanes(colour)],
            got0.at[chunk, :, lanes(colour)], rs_send.at[0, n], rs_recv.at[0, n], core_peer,
        )
        move.start()
        moves.append(move)
    small_step(0, core_peer)
    stage = []
    for n, (chunk, colour) in enumerate(items):
        moves[n].wait()
        shard1[chunk, :, lanes(colour)] = (
            part[chunk, piece(core * half, half), lanes(colour)].astype(F32)
            + got0[chunk, :, lanes(colour)].astype(F32)
        ).astype(BF16)
        (digit, peer), _ = orders(colour)
        move = remote(
            shard1.at[chunk, piece((1 - digit) * quarter, quarter), lanes(colour)],
            got1.at[chunk, :, lanes(colour)], rs_send.at[1, n], rs_recv.at[1, n], peer,
        )
        move.start()
        stage.append(move)
    small_step(1, y_peer)
    moves, stage = stage, []
    for n, (chunk, colour) in enumerate(items):
        moves[n].wait()
        (digit, _), (digit2, peer) = orders(colour)
        shard2[chunk, :, lanes(colour)] = (
            shard1[chunk, piece(digit * quarter, quarter), lanes(colour)].astype(F32)
            + got1[chunk, :, lanes(colour)].astype(F32)
        ).astype(BF16)
        move = remote(
            shard2.at[chunk, piece((1 - digit2) * eighth, eighth), lanes(colour)],
            got2.at[chunk, :, lanes(colour)], rs_send.at[2, n], rs_recv.at[2, n], peer,
        )
        move.start()
        stage.append(move)
    small_step(2, x_peer)
    moves, stage = stage, []
    for n, (chunk, colour) in enumerate(items):
        moves[n].wait()
        _, (digit2, _) = orders(colour)
        shard3[chunk, :, lanes(colour)] = (
            shard2[chunk, piece(digit2 * eighth, eighth), lanes(colour)].astype(F32)
            + got2[chunk, :, lanes(colour)].astype(F32)
        ).astype(BF16)
        for j in range(3):
            move = remote(
                shard3.at[chunk, piece(z_ids[j] * unit, unit), lanes(colour)],
                got3.at[chunk, j, :, lanes(colour)],
                rs_send.at[3 + j, n], rs_recv.at[3 + j, n], z_peers[j],
            )
            move.start()
            stage.append(move)
    z_moves = []
    for j in range(3):
        move = remote(small, small_got.at[3 + j], sm_send.at[3 + j], sm_recv.at[3 + j], z_peers[j])
        move.start()
        z_moves.append(move)
    for move in z_moves:
        move.wait()
    parts4 = [small[...]] + [small_got[3 + j] for j in range(3)]

    def by_place(place):
        total = None
        for j in range(4):
            term = jnp.where(lax.rem(zz - j + 4, 4) == place, parts4[j], 0.0)
            total = term if total is None else total + term
        return total

    small[...] = (by_place(0) + by_place(1)) + (by_place(2) + by_place(3))
    for e, peer in enumerate(w_peers):
        small_step(6 + e, peer)

    moves, stage = stage, []
    for n, (chunk, colour) in enumerate(items):
        total = shard3[chunk, piece(zz * unit, unit), lanes(colour)].astype(F32)
        for j in range(3):
            moves[3 * n + j].wait()
            total = total + got3[chunk, j, :, lanes(colour)].astype(F32)
        (digit, _), (digit2, _) = orders(colour)
        base = core * half + digit * quarter + digit2 * eighth
        mine = piece(base + zz * unit, unit)
        full[chunk, mine, lanes(colour)] = total.astype(BF16)
        for e, peer in enumerate(w_peers):
            move = remote(
                full.at[chunk, mine, lanes(colour)],
                got3.at[chunk, 3 + e, :, lanes(colour)],
                rs_send.at[6 + e, n], rs_recv.at[6 + e, n], peer,
            )
            move.start()
            move.wait()
            full[chunk, mine, lanes(colour)] = (
                full[chunk, mine, lanes(colour)].astype(F32)
                + got3[chunk, 3 + e, :, lanes(colour)].astype(F32)
            ).astype(BF16)
        for j in range(3):
            spot = full.at[chunk, mine, lanes(colour)]
            move = remote(spot, spot, ag_send.at[3 + j, n], ag_recv.at[3 + j, n], z_peers[j])
            move.start()
            stage.append(move)
    moves, stage = stage, []
    for n, (chunk, colour) in enumerate(items):
        for j in range(3):
            moves[3 * n + j].wait()
        (digit, _), (digit2, peer) = orders(colour)
        spot = full.at[chunk, piece(core * half + digit * quarter + digit2 * eighth, eighth), lanes(colour)]
        move = remote(spot, spot, ag_send.at[2, n], ag_recv.at[2, n], peer)
        move.start()
        stage.append(move)
    moves, stage = stage, []
    for n, (chunk, colour) in enumerate(items):
        moves[n].wait()
        (digit, peer), _ = orders(colour)
        spot = full.at[chunk, piece(core * half + digit * quarter, quarter), lanes(colour)]
        move = remote(spot, spot, ag_send.at[1, n], ag_recv.at[1, n], peer)
        move.start()
        stage.append(move)
    moves, stage = stage, []
    for n, (chunk, colour) in enumerate(items):
        moves[n].wait()
        spot = full.at[chunk, piece(core * half, half), lanes(colour)]
        move = remote(spot, spot, ag_send.at[0, n], ag_recv.at[0, n], core_peer)
        move.start()
        stage.append(move)
    finals = []
    for n, (chunk, colour) in enumerate(items):
        stage[n].wait()
        if colour == 2:
            final = pltpu.make_async_copy(full.at[chunk], grads_ref.at[chunk], fin_sem.at[chunk])
            final.start()
            finals.append(final)
    small_ref[...] = small[...]
    for move in out_moves:
        move.wait()
    pooled_ref[...] = pool[...]
    own_b.wait()
    own_i.wait()
    for final in finals:
        final.wait()


def finish_kernel(
    grads_ref, small_ref, pool_ref, bl_ref, ig_ref,
    block_ref, pooled_ref, igrad_ref, qkv_ref, qb_ref, vb_ref, out_ref, ob_ref, g1_ref, b1_ref,
    up_ref, ub_ref, down_ref, db_ref, g2_ref, b2_ref, sem,
):
    move1 = pltpu.make_async_copy(bl_ref, block_ref, sem.at[0])
    move2 = pltpu.make_async_copy(ig_ref, igrad_ref, sem.at[1])
    move1.start()
    move2.start()
    down_ref[...] = grads_ref[0].astype(F32)
    for i in range(4):
        up_ref[:, i * D : (i + 1) * D] = grads_ref[1, i * D : (i + 1) * D, :].astype(F32)
        ub_ref[:, i * D : (i + 1) * D] = small_ref[i : i + 1, :]
    out_ref[...] = grads_ref[2, :D, :].astype(F32)
    for i in range(3):
        qkv_ref[:, i * D : (i + 1) * D] = grads_ref[2, (i + 1) * D : (i + 2) * D, :].astype(F32)
    for m in range(4):
        pooled_ref[m] = pool_ref[m, :1, :]
    for row, ref in ((4, db_ref), (5, ob_ref), (6, qb_ref), (7, vb_ref), (8, g1_ref), (9, b1_ref), (10, g2_ref), (11, b2_ref)):
        ref[...] = small_ref[row : row + 1, :]
    move1.wait()
    move2.wait()


def body(
    ndp,
    inputs, lengths, cotangent, pool_cotangent, qkv_weight, query_bias, value_bias,
    out_weight, out_bias, norm1_gain, norm1_bias, up_weight, up_bias, down_weight,
    down_bias, norm2_gain, norm2_bias,
):
    any_spec = pl.BlockSpec(memory_space=pl.ANY)
    vmem = pl.BlockSpec(memory_space=pltpu.VMEM)
    smem = pl.BlockSpec(memory_space=pltpu.SMEM)
    extra = max(ndp.bit_length() - 4, 0)
    n_items = CHUNKS * 3

    def row(item):
        return item.reshape(1, -1)

    def v(*shape, dtype=BF16):
        return pltpu.VMEM(shape, dtype)

    dma = pltpu.SemaphoreType.DMA
    args = (
        inputs, lengths, cotangent, pool_cotangent,
        qkv_weight, row(query_bias), row(value_bias), out_weight, row(out_bias),
        row(norm1_gain), row(norm1_bias), up_weight, row(up_bias), down_weight, row(down_bias),
        row(norm2_gain), row(norm2_bias),
    )
    in_specs = [
        any_spec, smem, any_spec, vmem,
        any_spec, vmem, vmem, any_spec, vmem,
        vmem, vmem, any_spec, vmem, any_spec, vmem,
        vmem, vmem,
    ]
    results = pl.pallas_call(
        functools.partial(kernel, ndp),
        out_shape=(
            jax.ShapeDtypeStruct(inputs.shape, BF16),
            jax.ShapeDtypeStruct((4, 8, D), F32),
            jax.ShapeDtypeStruct(inputs.shape, BF16),
            jax.ShapeDtypeStruct((CHUNKS, ROWS, D), BF16),
            jax.ShapeDtypeStruct((16, D), F32),
        ),
        in_specs=in_specs,
        out_specs=(any_spec, vmem, any_spec, any_spec, vmem),
        scratch_shapes=[
            v(512, D), v(512, D), v(D, 3 * D), v(D, D), v(D, FF), v(FF, D), v(3 * D, D), v(D + 16, 512),
            v(D, 512), v(D, 512), v(D, 512), v(H * VROWS, 512), v(H, 512, 512), v(H, 8, 512, dtype=F32),
            v(D, 512), v(512, D, dtype=F32), v(512, 1, dtype=F32), v(512, D), v(512, FF), v(512, FF, dtype=F32),
            v(512, D, dtype=F32), v(512, D, dtype=F32), v(512, D), v(512, FF), v(512, D, dtype=F32),
            v(D, 512), v(3 * D, 512), v(512, D), v(512, D), v(4, 8, D, dtype=F32),
            v(CHUNKS, ROWS, D), v(CHUNKS, ROWS // 2, D), v(CHUNKS, ROWS // 4, D), v(CHUNKS, ROWS // 8, D),
            v(CHUNKS, 3 + extra, ROWS // 32, D),
            v(CHUNKS, ROWS // 2, D), v(CHUNKS, ROWS // 4, D), v(CHUNKS, ROWS // 8, D),
            v(CHUNKS, ROWS, D), v(16, D, dtype=F32), v(6 + extra, 16, D, dtype=F32),
            dma((4,)), dma((4,)), dma((2, 3)), dma((2, 3)), dma((2, 3)), dma((2, 3)), dma((3,)), dma((3,)),
            dma((6 + extra, n_items)), dma((6 + extra, n_items)), dma((6, n_items)), dma((6, n_items)),
            dma((6 + extra,)), dma((6 + extra,)), dma((CHUNKS,)),
        ],
        compiler_params=pltpu.CompilerParams(
            collective_id=0, has_side_effects=True, vmem_limit_bytes=58 * 2**20
        ),
    )(*args)
    block, pooled, igrad, grads, small = results

    def shape(*dims, dtype=F32):
        return jax.ShapeDtypeStruct(dims, dtype)

    outs = pl.pallas_call(
        finish_kernel,
        out_shape=(
            shape(*inputs.shape, dtype=BF16), shape(4, 1, D), shape(*inputs.shape, dtype=BF16),
            shape(D, 3 * D), shape(1, D), shape(1, D), shape(D, D), shape(1, D), shape(1, D), shape(1, D),
            shape(D, FF), shape(1, FF), shape(FF, D), shape(1, D), shape(1, D), shape(1, D),
        ),
        in_specs=[vmem, vmem, vmem, any_spec, any_spec],
        out_specs=(any_spec, vmem, any_spec) + (vmem,) * 13,
        scratch_shapes=[dma((2,))],
        compiler_params=pltpu.CompilerParams(vmem_limit_bytes=40 * 2**20),
    )(grads, small, pooled, block, igrad)
    outs = list(outs)
    for i in (4, 5, 7, 8, 9, 11, 13, 14, 15):
        outs[i] = outs[i].reshape(-1)
    return tuple(outs)


def solution(mesh):
    whole = P()
    return jax.shard_map(
        functools.partial(body, mesh.shape["dp"]),
        mesh=mesh,
        in_specs=(
            P(None, "dp", "seq", None), P(None, "dp"), P(None, "dp", "seq", None), P(None, "dp", None),
        ) + (whole,) * 13,
        out_specs=(
            P(None, "dp", "seq", None), P(None, "dp", None), P(None, "dp", "seq", None),
        ) + (whole,) * 13,
        check_vma=False,
    )
```

time: 534 us -> 138 us (0.26); the launches traced: 528 us -> 137 us
  waiting for transfers between devices: 188 us -> 0 us
  Pallas kernels: 0 us -> 112 us
  blocking collectives: 108 us -> 0 us
  matrix products: 94.8 us -> 0 us
  local copies, waits for them, and re-layouts: 80.4 us -> 19.4 us
  other arithmetic: 35.3 us -> 5.38 us
  between operations: 19.9 us -> 0.68 us
    psum x1 -> x0, waiting for transfers between devices: 122 us -> none  [body(): totals = lax.psum(totals, ('dp', 'seq'))]
    pallas_call x0 -> x2, Pallas kernels: none -> 112 us  [the longest x1 108 us: body(): pl.pallas_call(functools.partial(kernel, ndp), out_shape=(jax.ShapeDtypeS...]
    dot_general x72 -> x0, matrix products: 94.8 us -> none  [the longest x4 10.7 us: attend_back(): jnp.einsum('bhqk,bqhd->bkhd', probs.astype(jnp.bfloat16), grad_context, p...]
    unnamed x17 -> x0, waiting for transfers between devices: 65.9 us -> none
    all_gather x8 -> x0, blocking collectives: 58.3 us -> none  [the longest x4 30.2 us: body(): lax.all_gather(keys_here, 'seq', axis=1, tiled=True)]
    unnamed x456 -> x12, local copies, waits for them, and re-layouts: 62.7 us -> 8.11 us
    psum x2 -> x0, blocking collectives: 49.9 us -> none  [the longest x1 41.7 us: body(): totals = lax.psum(totals, ('dp', 'seq'))]
    reduce_sum x26 -> x0, other arithmetic: 12 us -> none  [the longest x4 3.68 us: attend_block(): total = jnp.sum(raised, axis=-1, keepdims=True)]
  transfers between devices with their start and end apart: 9 -> 0, of which waited for: 4 -> 0; matrix products, arithmetic and copies ran while one was open for 20% -> 0% of each run, Pallas kernels for 0% -> 0%
where the time goes in v1:
time: 138 us; the launch traced here: 137 us
  Pallas kernels  112 us (81%)
  local copies, waits for them, and re-layouts  19.4 us (14%)
  other arithmetic  5.38 us (4%)
    pallas_call x1, Pallas kernels, body(): pl.pallas_call(functools.partial(kernel, ndp), out_shape=(jax.ShapeDtypeS...  108 us
    reshape x9, local copies, waits for them, and re-layouts, row(): return item.reshape(1, -1)  11.2 us
    unnamed x12, local copies, waits for them, and re-layouts  8.11 us
    pallas_call x9, other arithmetic, body(): pl.pallas_call(finish_kernel, out_shape=(shape(*inputs.shape, dtype=BF16)...  5.38 us
    pallas_call x1, Pallas kernels, body(): pl.pallas_call(finish_kernel, out_shape=(shape(*inputs.shape, dtype=BF16)...  3.85 us

profile of v1, /device:TPU:0, one launch (start us, length us, event | category | flops | bytes accessed | tf_op | source)
XLA Modules:
  0.0 137.4 jit_solution(3305087897348472491)
XLA Ops:
  0.6 1.2 reshape.86.qb_ref
  1.9 1.2 reshape.87.vb_ref
  3.1 1.2 reshape.88.ob_ref
  4.4 1.2 reshape.89.g1_ref
  5.6 1.2 reshape.90.b1_ref
  6.9 1.2 reshape.92.db_ref
  8.1 1.2 reshape.93.g2_ref
  9.4 1.2 reshape.94.b2_ref
  10.6 1.3 copy.33.lengths_ref
  11.9 1.3 copy.34.pool_ref
  13.2 1.3 reshape.91.ub_ref
  14.5 108.1 %shard_map.288 = (bf16[4,1,128,384]{3,2,1,0:T(8,128)(2,1)}, f32[4,8,384]{2,1,0:T(8,128)}, bf16[4,1,128,384]{3,2,1,0:T(8,128)(2,1)}, bf16[3,1536,384]{2,1,0:T(8,128)(2,1)}, f32[16,384]{1,0:T(8,128)}) custom-call(bf16[4,1,128,384]{3,2,1,0:T(8,128)(2,1)} %inputs_ref.1, s32[4,1]{1,0:T(4,128)} %copy.33.lengths_ref, bf16[4,1,128,384]{3,2,1,0:T(8,128)(2,1)} %cot_ref.1, ...), custom_call_target="tpu_custom_call" | custom-call | tf_op jit(solution)/shard_map/pallas_call | solution.py:545
  122.6 0.0 copy-start
  122.6 2.0 %copy-done = bf16[3,1536,384]{2,1,0:T(8,128)(2,1)S(1)} copy-done((bf16[3,1536,384]{2,1,0:T(8,128)(2,1)S(1)}, bf16[3,1536,384]{2,1,0:T(8,128)(2,1)}, u32[]{:S(2)}) %copy-start) | copy-done | bytes 3538968
  124.6 0.0 copy-start.1
  124.6 1.0 copy-done.1
  125.6 0.0 copy-start.2
  125.6 1.0 copy-done.2
  126.6 0.0 copy-start.3
  126.6 0.8 copy-done.3
  127.4 0.0 copy-start.4
  127.4 0.7 copy-done.4
  128.1 3.9 %shard_map.289 = (bf16[4,1,128,384]{3,2,1,0:T(8,128)(2,1)}, f32[4,1,384]{2,1,0:T(1,128)}, bf16[4,1,128,384]{3,2,1,0:T(8,128)(2,1)}, f32[384,1152]{1,0:T(8,128)},...) custom-call(bf16[3,1536,384]{2,1,0:T(8,128)(2,1)S(1)} %copy-done, ...), custom_call_target="tpu_custom_call" | custom-call | tf_op jit(solution)/shard_map/pallas_call | solution.py:579
  132.0 0.6 reduce
  132.6 0.6 reduce.1
  133.2 0.6 reduce.2
  133.8 0.6 reduce.3
  134.4 0.6 reduce.4
  134.9 0.6 reduce.6
  135.5 0.6 reduce.7
  136.1 0.6 reduce.8
  136.7 0.6 reduce.5
Async XLA Ops:
  122.6 2.0 %copy-start = (bf16[3,1536,384]{2,1,0:T(8,128)(2,1)S(1)}, bf16[3,1536,384]{2,1,0:T(8,128)(2,1)}, u32[]{:S(2)}) copy-start(bf16[3,1536,384]{2,1,0:T(8,128)(2,1)} %get-tuple-element.37.grads_ref) | copy-start | bytes 10616836
  124.6 1.0 copy-start.1
  125.6 1.0 copy-start.2
  126.6 0.8 copy-start.3
  127.4 0.7 copy-start.4

commit v2 on v1

--- a/solution.py
+++ b/solution.py
@@ -59,7 +59,7 @@
     x, cot, qkv_w, out_w, up_w, down_w, qkv_t, x_t,
     q_t, kd_t, kz_t, v_x, probs, inv, c_t, y1, r1, first_low, active, slope,
     lower, gsum, g_low, g_up, g_hid, gc_t, gj_t, bout, igr, pool,
-    part, got0, got1, got2, got3, shard1, shard2, shard3, full, small, small_got,
+    part, got0, got1, got2, got3, shard1, shard2, shard3, full, small, small_got, up_row,
     w_sem, loc_sem, in_send, in_recv, out_send, out_recv, pool_send, pool_recv,
     rs_send, rs_recv, ag_send, ag_recv, sm_send, sm_recv, fin_sem,
 ):
@@ -123,7 +123,12 @@
             move.start()
             moves.append(move)
 
-    span = lengths_ref[sq, 0]
+    span = lengths_ref[0, sq]
+    query_bias, value_bias, out_bias, gain_one, bias_one, up_bias, down_bias, gain_two, bias_two = (
+        ref[...].reshape(1, -1)
+        for ref in (qb_ref, vb_ref, ob_ref, g1_ref, b1_ref, ub_ref, db_ref, g2_ref, b2_ref)
+    )
+    up_row[...] = up_bias
     count = span.astype(F32)
     lane_valid = lax.broadcasted_iota(jnp.int32, (1, 512), 1) < span
 
@@ -142,8 +147,8 @@
     x_t[:D, :] = x[...].T
     x_t[D:, :] = jnp.ones((16, 512), BF16)
 
-    qcol = jnp.broadcast_to(qb_ref[...], (8, D)).T[:, :1]
-    vcol = jnp.broadcast_to(vb_ref[...], (8, D)).T[:, :1]
+    qcol = jnp.broadcast_to(query_bias, (8, D)).T[:, :1]
+    vcol = jnp.broadcast_to(value_bias, (8, D)).T[:, :1]
     q_t[...] = (dot(qkv_t[:D, :], x[...], NT) + qcol).astype(BF16)
     keys = dot(qkv_t[D : 2 * D, :], x[...], NT)
     kd_t[...] = jnp.where(lane_valid, keys, keys[:, :1]).astype(BF16)
@@ -177,10 +182,10 @@
 
     def norm_one(i, carry):
         rows = rows_of(i, 128)
-        normal, inverse = layer_norm(x[rows, :].astype(F32) + lower[rows, :] + ob_ref[...])
+        normal, inverse = layer_norm(x[rows, :].astype(F32) + lower[rows, :] + out_bias)
         y1[rows, :] = normal
         r1[rows, :] = inverse
-        first_low[rows, :] = (normal * g1_ref[...] + b1_ref[...]).astype(BF16)
+        first_low[rows, :] = (normal * gain_one + bias_one).astype(BF16)
         return carry
 
     lax.fori_loop(0, 4, norm_one, 0)
@@ -188,7 +193,7 @@
 
     def raise_up(i, carry):
         cols = rows_of(i, 256)
-        upper = dot(first_low[...], up_w[:, cols], NN) + ub_ref[:, cols]
+        upper = dot(first_low[...], up_w[:, cols], NN) + up_row[:, cols]
         act, slp = gelu_and_slope(upper)
         active[:, cols] = act.astype(BF16)
         slope[:, cols] = slp
@@ -200,20 +205,21 @@
     own_c.wait()
     for move in c_moves:
         move.wait()
-    pool_share = pool_ref[sq].astype(F32) / count
+    chosen = lax.broadcasted_iota(jnp.int32, (4, D), 0) == sq
+    pool_share = jnp.sum(jnp.where(chosen, pool_ref[0].astype(F32), 0.0), axis=0, keepdims=True) / count
 
     zero_row = jnp.zeros((1, D), F32)
 
     def norm_two(i, carry):
         sums, gain_sum, bias_sum, down_sum = carry
         rows = rows_of(i, 128)
-        firsts = y1[rows, :] * g1_ref[...] + b1_ref[...]
-        normal, inverse = layer_norm(firsts + lower[rows, :] + db_ref[...])
+        firsts = y1[rows, :] * gain_one + bias_one
+        normal, inverse = layer_norm(firsts + lower[rows, :] + down_bias)
         here = lax.broadcasted_iota(jnp.int32, (128, 1), 0) + i * 128 < span
-        masked = jnp.where(here, normal * g2_ref[...] + b2_ref[...], 0.0)
+        masked = jnp.where(here, normal * gain_two + bias_two, 0.0)
         bout[rows, :] = masked.astype(BF16)
         grad = jnp.where(here, cot[rows, :].astype(F32) + pool_share, 0.0)
-        grad_in = norm_back(grad, normal, inverse, g2_ref[...])
+        grad_in = norm_back(grad, normal, inverse, gain_two)
         gsum[rows, :] = grad_in
         low = grad_in.astype(BF16)
         g_low[rows, :] = low
@@ -269,7 +275,7 @@
         rows = rows_of(i, 128)
         grad = gsum[rows, :] + lower[rows, :]
         normal = y1[rows, :]
-        grad_in = norm_back(grad, normal, r1[rows, :], g1_ref[...])
+        grad_in = norm_back(grad, normal, r1[rows, :], gain_one)
         g_hid[rows, :] = grad_in
         low = grad_in.astype(BF16)
         g_low[rows, :] = low
@@ -490,25 +496,49 @@
 def finish_kernel(
     grads_ref, small_ref, pool_ref, bl_ref, ig_ref,
     block_ref, pooled_ref, igrad_ref, qkv_ref, qb_ref, vb_ref, out_ref, ob_ref, g1_ref, b1_ref,
-    up_ref, ub_ref, down_ref, db_ref, g2_ref, b2_ref, sem,
+    up_ref, ub_ref, down_ref, db_ref, g2_ref, b2_ref,
+    low, wide, held, in_sem, out_sem, sem,
 ):
-    move1 = pltpu.make_async_copy(bl_ref, block_ref, sem.at[0])
-    move2 = pltpu.make_async_copy(ig_ref, igrad_ref, sem.at[1])
-    move1.start()
-    move2.start()
-    down_ref[...] = grads_ref[0].astype(F32)
+    moves, loads = [], []
+    for i in range(12):
+        load = pltpu.make_async_copy(
+            grads_ref.at[i // 4, pl.ds((i % 4) * D, D)], low.at[i], in_sem.at[i]
+        )
+        load.start()
+        loads.append(load)
+    passes = ((bl_ref, block_ref), (ig_ref, igrad_ref))
+    for i, (src, _) in enumerate(passes):
+        load = pltpu.make_async_copy(src, held.at[i], sem.at[i])
+        load.start()
+        loads.append(load)
     for i in range(4):
-        up_ref[:, i * D : (i + 1) * D] = grads_ref[1, i * D : (i + 1) * D, :].astype(F32)
-        ub_ref[:, i * D : (i + 1) * D] = small_ref[i : i + 1, :]
-    out_ref[...] = grads_ref[2, :D, :].astype(F32)
-    for i in range(3):
-        qkv_ref[:, i * D : (i + 1) * D] = grads_ref[2, (i + 1) * D : (i + 2) * D, :].astype(F32)
+        ub_ref[i * D : (i + 1) * D] = small_ref[i, :]
     for m in range(4):
         pooled_ref[m] = pool_ref[m, :1, :]
     for row, ref in ((4, db_ref), (5, ob_ref), (6, qb_ref), (7, vb_ref), (8, g1_ref), (9, b1_ref), (10, g2_ref), (11, b2_ref)):
-        ref[...] = small_ref[row : row + 1, :]
-    move1.wait()
-    move2.wait()
+        ref[...] = small_ref[row, :]
+    for i in range(12):
+        loads[i].wait()
+        wide[i] = low[i].astype(F32)
+        span = pl.ds((i % 4) * D, D)
+        if i < 4:
+            place = down_ref.at[span]
+        elif i < 8:
+            place = up_ref.at[:, span]
+        elif i == 8:
+            place = out_ref
+        else:
+            place = qkv_ref.at[:, pl.ds((i - 9) * D, D)]
+        move = pltpu.make_async_copy(wide.at[i], place, out_sem.at[i])
+        move.start()
+        moves.append(move)
+    for i, (_, dst) in enumerate(passes):
+        loads[12 + i].wait()
+        move = pltpu.make_async_copy(held.at[i], dst, sem.at[2 + i])
+        move.start()
+        moves.append(move)
+    for move in moves:
+        move.wait()
 
 
 def body(
@@ -517,24 +547,21 @@
     out_weight, out_bias, norm1_gain, norm1_bias, up_weight, up_bias, down_weight,
     down_bias, norm2_gain, norm2_bias,
 ):
-    any_spec = pl.BlockSpec(memory_space=pl.ANY)
+    any_spec = pl.BlockSpec(memory_space=pltpu.HBM)
     vmem = pl.BlockSpec(memory_space=pltpu.VMEM)
     smem = pl.BlockSpec(memory_space=pltpu.SMEM)
     extra = max(ndp.bit_length() - 4, 0)
     n_items = CHUNKS * 3
 
-    def row(item):
-        return item.reshape(1, -1)
-
     def v(*shape, dtype=BF16):
         return pltpu.VMEM(shape, dtype)
 
     dma = pltpu.SemaphoreType.DMA
     args = (
-        inputs, lengths, cotangent, pool_cotangent,
-        qkv_weight, row(query_bias), row(value_bias), out_weight, row(out_bias),
-        row(norm1_gain), row(norm1_bias), up_weight, row(up_bias), down_weight, row(down_bias),
-        row(norm2_gain), row(norm2_bias),
+        inputs, lengths.T, cotangent, jnp.transpose(pool_cotangent, (1, 0, 2)),
+        qkv_weight, query_bias, value_bias, out_weight, out_bias,
+        norm1_gain, norm1_bias, up_weight, up_bias, down_weight, down_bias,
+        norm2_gain, norm2_bias,
     )
     in_specs = [
         any_spec, smem, any_spec, vmem,
@@ -562,7 +589,7 @@
             v(CHUNKS, ROWS, D), v(CHUNKS, ROWS // 2, D), v(CHUNKS, ROWS // 4, D), v(CHUNKS, ROWS // 8, D),
             v(CHUNKS, 3 + extra, ROWS // 32, D),
             v(CHUNKS, ROWS // 2, D), v(CHUNKS, ROWS // 4, D), v(CHUNKS, ROWS // 8, D),
-            v(CHUNKS, ROWS, D), v(16, D, dtype=F32), v(6 + extra, 16, D, dtype=F32),
+            v(CHUNKS, ROWS, D), v(16, D, dtype=F32), v(6 + extra, 16, D, dtype=F32), v(1, FF, dtype=F32),
             dma((4,)), dma((4,)), dma((2, 3)), dma((2, 3)), dma((2, 3)), dma((2, 3)), dma((3,)), dma((3,)),
             dma((6 + extra, n_items)), dma((6 + extra, n_items)), dma((6, n_items)), dma((6, n_items)),
             dma((6 + extra,)), dma((6 + extra,)), dma((CHUNKS,)),
@@ -580,18 +607,18 @@
         finish_kernel,
         out_shape=(
             shape(*inputs.shape, dtype=BF16), shape(4, 1, D), shape(*inputs.shape, dtype=BF16),
-            shape(D, 3 * D), shape(1, D), shape(1, D), shape(D, D), shape(1, D), shape(1, D), shape(1, D),
-            shape(D, FF), shape(1, FF), shape(FF, D), shape(1, D), shape(1, D), shape(1, D),
+            shape(D, 3 * D), shape(D), shape(D), shape(D, D), shape(D), shape(D), shape(D),
+            shape(D, FF), shape(FF), shape(FF, D), shape(D), shape(D), shape(D),
         ),
-        in_specs=[vmem, vmem, vmem, any_spec, any_spec],
-        out_specs=(any_spec, vmem, any_spec) + (vmem,) * 13,
-        scratch_shapes=[dma((2,))],
-        compiler_params=pltpu.CompilerParams(vmem_limit_bytes=40 * 2**20),
+        in_specs=[any_spec, vmem, vmem, any_spec, any_spec],
+        out_specs=(
+            any_spec, vmem, any_spec, any_spec, vmem, vmem, any_spec, vmem, vmem, vmem,
+            any_spec, vmem, any_spec, vmem, vmem, vmem,
+        ),
+        scratch_shapes=[v(12, D, D), v(12, D, D, dtype=F32), v(2, *inputs.shape), dma((12,)), dma((12,)), dma((4,))],
+        compiler_params=pltpu.CompilerParams(vmem_limit_bytes=58 * 2**20),
     )(grads, small, pooled, block, igrad)
-    outs = list(outs)
-    for i in (4, 5, 7, 8, 9, 11, 13, 14, 15):
-        outs[i] = outs[i].reshape(-1)
-    return tuple(outs)
+    return outs
 
 
 def solution(mesh):

time: 138 us -> 115 us (0.83)
  local copies, waits for them, and re-layouts: 19.4 us -> 0 us
  other arithmetic: 5.38 us -> 0 us
  Pallas kernels: 112 us -> 114 us
    reshape x9 -> x0, local copies, waits for them, and re-layouts: 11.2 us -> none  [row(): return item.reshape(1, -1)]
    unnamed x12 -> x0, local copies, waits for them, and re-layouts: 8.11 us -> none
    pallas_call x9 -> x0, other arithmetic: 5.38 us -> none  [body(): pl.pallas_call(finish_kernel, out_shape=(shape(*inputs.shape, dtype=BF16)...]
    pallas_call x1, Pallas kernels: 3.85 us -> 5.83 us  [body(): pl.pallas_call(finish_kernel, out_shape=(shape(*inputs.shape, dtype=BF16)...]
where the time goes in v2:
time: 115 us
  Pallas kernels  114 us (99%)
    pallas_call x1, Pallas kernels, body(): pl.pallas_call(functools.partial(kernel, ndp), out_shape=(jax.ShapeDtypeS...  108 us
    pallas_call x1, Pallas kernels, body(): pl.pallas_call(finish_kernel, out_shape=(shape(*inputs.shape, dtype=BF16)...  5.83 us

profile of v2, /device:TPU:0, one launch (start us, length us, event | category | flops | bytes accessed | tf_op | source)
XLA Modules:
  0.0 114.6 jit_solution(15674104122311515371)
XLA Ops:
  0.7 108.1 %shard_map.288 = (bf16[4,1,128,384]{3,2,1,0:T(8,128)(2,1)}, f32[4,8,384]{2,1,0:T(8,128)}, bf16[4,1,128,384]{3,2,1,0:T(8,128)(2,1)}, bf16[3,1536,384]{2,1,0:T(8,128)(2,1)}, f32[16,384]{1,0:T(8,128)}) custom-call(bf16[4,1,128,384]{3,2,1,0:T(8,128)(2,1)} %inputs_ref.1, s32[1,4]{1,0:T(1,128)} %bitcast.3, bf16[4,1,128,384]{3,2,1,0:T(8,128)(2,1)} %cot_ref.1, ...), custom_call_target="tpu_custom_call" | custom-call | tf_op jit(solution)/shard_map/pallas_call | solution.py:572
  108.8 5.8 %shard_map.289 = (bf16[4,1,128,384]{3,2,1,0:T(8,128)(2,1)}, f32[4,1,384]{2,1,0:T(1,128)}, bf16[4,1,128,384]{3,2,1,0:T(8,128)(2,1)}, f32[384,1152]{1,0:T(8,128)},...) custom-call(bf16[3,1536,384]{2,1,0:T(8,128)(2,1)} %get-tuple-element, ...), custom_call_target="tpu_custom_call" | custom-call | tf_op jit(solution)/shard_map/pallas_call | solution.py:606

commit v3 on v2

v3 whole, which is shorter than its diff:
```python
import functools

import jax
import jax.numpy as jnp
from jax import lax
from jax.experimental import pallas as pl
from jax.experimental.pallas import tpu as pltpu
from jax.sharding import PartitionSpec as P

H = 12
HD = 32
D = 384
FF = 1536
EPS = 1e-6
F32 = jnp.float32
BF16 = jnp.bfloat16
MESH = pl.DeviceIdType.MESH
NN = (((1,), (0,)), ((), ()))
NT = (((1,), (1,)), ((), ()))
TN = (((0,), (0,)), ((), ()))
LOG2E = 1.4426950408889634
SCALE = HD**-0.5
VROWS = HD + 16
CHUNKS = 3
ROWS = 1536
GROUPS = 3
ORDERS = (
    ("x", "y", "z1", "z2"), ("y", "x", "z1", "z2"), ("z1", "z2", "x", "y"),
    ("x", "y", "z1", "z2"), ("y", "x", "z1", "z2"), ("z1", "z2", "x", "y"),
)
HALVE_TIMES = (0.0, 1.5, 5.5, 8.5, 11.0, 13.5, 16.0, 18.5, 21.0, 24.5, 25.5)
SPREAD_TIMES = (0.0, 1.2, 5.5, 10.5, 14.5, 16.5)
VECTOR_TIMES = (0.0, 1.2, 4.0, 6.8, 10.5)


def dot(left, right, dims):
    return lax.dot_general(left, right, dims, preferred_element_type=F32)


def gelu_and_slope(upper):
    cdf = 0.5 * (1.0 + lax.erf(upper * 2.0**-0.5))
    density = jnp.exp2((-0.5 * LOG2E) * (upper * upper)) * (2.0 * jnp.pi) ** -0.5
    return upper * cdf, cdf + upper * density


def layer_norm(values):
    centre = values - jnp.mean(values, axis=-1, keepdims=True)
    inverse = lax.rsqrt(jnp.mean(centre * centre, axis=-1, keepdims=True) + EPS)
    return centre * inverse, inverse


def norm_back(grad_out, normal, inverse, gain):
    scaled = grad_out * gain
    return inverse * (
        scaled
        - jnp.mean(scaled, axis=-1, keepdims=True)
        - normal * jnp.mean(scaled * normal, axis=-1, keepdims=True)
    )


def kernel(
    ndp,
    inputs_ref, lengths_ref, cot_ref, pool_ref,
    qkv_hbm, qb_ref, vb_ref, out_hbm, ob_ref, g1_ref, b1_ref,
    up_hbm, ub_ref, down_hbm, db_ref, g2_ref, b2_ref,
    block_ref, pooled_ref, igrad_ref, full, small_ref,
    x, cot, qkv_w, out_w, up_w, down_w, qkv_t, x_t,
    q_t, kd_t, kz_t, v_x, probs, inv, c_t, y1, r1, first_low, active, slope,
    lower, gsum, g_low, g_up, g_hid, gc_t, gj_t, bout, igr, pool,
    part, got0, got1, got2, got3, got4, sum0, sum1, sum2, sum3, blk0, blk1, blk2, blk_sum,
    small, small_got, small_z, up_row,
    w_sem, loc_sem, in_send, in_recv, out_send, out_recv, pool_send, pool_recv,
    rs_send, rs_recv, ag_send, ag_recv, blk_send, blk_recv, sm_send, sm_recv,
):
    dp = lax.axis_index("dp")
    sq = lax.axis_index("seq")
    core = lax.rem(sq, 2)
    yy = lax.div(sq, 2)
    xx = lax.rem(dp, 2)
    zz = lax.rem(lax.div(dp, 2), 4)
    extra = []
    bit = 8
    while bit < ndp:
        extra.append(bit)
        bit *= 2

    def flip(index, amount):
        digit = lax.rem(lax.div(index, amount), 2)
        return index + amount * (1 - 2 * digit)

    seq_peers = [lax.rem(sq + step, 4) for step in (1, 2, 3)]
    core_peer = (dp, flip(sq, 1))
    y_peer = (dp, flip(sq, 2))
    x_peer = (flip(dp, 1), sq)
    xy_peer = (flip(dp, 1), flip(sq, 2))
    z_peers = [(dp + 2 * (lax.rem(zz + step, 4) - zz), sq) for step in (1, 2, 3)]
    w_peers = [(flip(dp, amount), sq) for amount in extra]
    greeted = [(dp, peer) for peer in seq_peers] + [x_peer, xy_peer] + z_peers + w_peers
    halvings = {
        "core": (core, core_peer),
        "y": (yy, y_peer),
        "x": (xx, x_peer),
        "z1": (lax.rem(zz, 2), (flip(dp, 2), sq)),
        "z2": (lax.div(zz, 2), (flip(dp, 4), sq)),
    }

    loads = [
        pltpu.make_async_copy(src, dst, w_sem.at[i])
        for i, (src, dst) in enumerate(
            [(qkv_hbm, qkv_w), (out_hbm, out_w), (up_hbm, up_w), (down_hbm, down_w)]
        )
    ]
    for load in loads:
        load.start()
    own_rows = pl.ds(pl.multiple_of(sq * 128, 128), 128)
    own_x = pltpu.make_async_copy(inputs_ref.at[sq, 0], x.at[own_rows], loc_sem.at[0])
    own_c = pltpu.make_async_copy(cot_ref.at[sq, 0], cot.at[own_rows], loc_sem.at[1])
    own_x.start()
    own_c.start()

    barrier = pltpu.get_barrier_semaphore()
    for peer in greeted:
        pl.semaphore_signal(barrier, inc=1, device_id=peer, device_id_type=MESH)
    pl.semaphore_wait(barrier, len(greeted))

    def remote(src, dst, send, recv, peer):
        return pltpu.make_async_remote_copy(
            src_ref=src, dst_ref=dst, send_sem=send, recv_sem=recv,
            device_id=peer, device_id_type=MESH,
        )

    x_moves, c_moves = [], []
    for which, (src, dst, moves) in enumerate(((inputs_ref, x, x_moves), (cot_ref, cot, c_moves))):
        for i, peer in enumerate(seq_peers):
            move = remote(
                src.at[peer, 0], dst.at[own_rows],
                in_send.at[which, i], in_recv.at[which, i], (dp, peer),
            )
            moves.append(move)
    for move in x_moves:
        move.start()

    span = lengths_ref[0, sq]
    query_bias, value_bias, out_bias, gain_one, bias_one, up_bias, down_bias, gain_two, bias_two = (
        ref[...].reshape(1, -1)
        for ref in (qb_ref, vb_ref, ob_ref, g1_ref, b1_ref, ub_ref, db_ref, g2_ref, b2_ref)
    )
    up_row[...] = up_bias
    count = span.astype(F32)
    lane_valid = lax.broadcasted_iota(jnp.int32, (1, 512), 1) < span

    loads[0].wait()

    for i in range(3):
        for g in range(GROUPS):
            qkv_t[g * D + i * 128 : g * D + (i + 1) * 128, :] = qkv_w[:, i * D + g * 128 : i * D + (g + 1) * 128].T
    own_x.wait()
    for move in x_moves:
        move.wait()
    for move in c_moves:
        move.start()

    x_t[:D, :] = x[...].T
    x_t[D:, :] = jnp.ones((16, 512), BF16)

    qcol = jnp.broadcast_to(query_bias, (8, D)).T[:, :1]
    vcol = jnp.broadcast_to(value_bias, (8, D)).T[:, :1]
    ones_row = jnp.broadcast_to(jnp.where(lane_valid, 1.0, 0.0), (16, 512)).astype(BF16)
    for g in range(GROUPS):
        feats = slice(g * 128, (g + 1) * 128)
        joined = dot(qkv_t[g * D : (g + 1) * D, :], x[...], NT)
        q_t[feats, :] = (joined[:128] + qcol[feats]).astype(BF16)
        keys = joined[128:256]
        kd_t[feats, :] = jnp.where(lane_valid, keys, keys[:, :1]).astype(BF16)
        kz_t[feats, :] = jnp.where(lane_valid, keys, 0.0).astype(BF16)
        values = jnp.where(lane_valid, joined[256:] + vcol[feats], 0.0).astype(BF16)
        for i in range(4):
            h = 4 * g + i
            v_x[h * VROWS : h * VROWS + HD, :] = values[i * HD : (i + 1) * HD, :]
            v_x[h * VROWS + HD : (h + 1) * VROWS, :] = ones_row

    def attend(h, carry):
        rows = pl.ds(pl.multiple_of(h * HD, HD), HD)
        scores = dot(kd_t[rows, :], q_t[rows, :], TN)
        peak = jnp.max(scores, axis=0, keepdims=True)
        raised = jnp.exp2(scores * (SCALE * LOG2E) - peak * (SCALE * LOG2E)).astype(BF16)
        probs[h] = raised
        both = dot(v_x[pl.ds(pl.multiple_of(h * VROWS, 16), VROWS), :], raised, NN)
        inverse = 1.0 / both[HD : HD + 1, :]
        inv[h] = jnp.broadcast_to(inverse, (8, 512))
        c_t[rows, :] = (both[:HD, :] * inverse).astype(BF16)
        return carry

    lax.fori_loop(0, H, attend, 0, unroll=4)

    loads[1].wait()

    def rows_of(i, size):
        return pl.ds(pl.multiple_of(i * size, size), size)

    lower[...] = dot(c_t[...], out_w[...], TN)

    def norm_one(i, carry):
        rows = rows_of(i, 128)
        normal, inverse = layer_norm(x[rows, :].astype(F32) + lower[rows, :] + out_bias)
        y1[rows, :] = normal
        r1[rows, :] = inverse
        first_low[rows, :] = (normal * gain_one + bias_one).astype(BF16)
        return carry

    lax.fori_loop(0, 4, norm_one, 0)
    loads[2].wait()

    def raise_up(i, carry):
        cols = rows_of(i, 256)
        upper = dot(first_low[...], up_w[:, cols], NN) + up_row[:, cols]
        act, slp = gelu_and_slope(upper)
        active[:, cols] = act.astype(BF16)
        slope[:, cols] = slp
        return carry

    lax.fori_loop(0, FF // 256, raise_up, 0)
    loads[3].wait()
    lower[...] = dot(active[...], down_w[...], NN)
    own_c.wait()
    for move in c_moves:
        move.wait()
    chosen = lax.broadcasted_iota(jnp.int32, (4, D), 0) == sq
    pool_share = jnp.sum(jnp.where(chosen, pool_ref[0].astype(F32), 0.0), axis=0, keepdims=True) / count

    zero_row = jnp.zeros((1, D), F32)

    def norm_two(i, carry):
        sums, gain_sum, bias_sum, down_sum = carry
        rows = rows_of(i, 128)
        firsts = y1[rows, :] * gain_one + bias_one
        normal, inverse = layer_norm(firsts + lower[rows, :] + down_bias)
        here = lax.broadcasted_iota(jnp.int32, (128, 1), 0) + i * 128 < span
        masked = jnp.where(here, normal * gain_two + bias_two, 0.0)
        bout[rows, :] = masked.astype(BF16)
        grad = jnp.where(here, cot[rows, :].astype(F32) + pool_share, 0.0)
        grad_in = norm_back(grad, normal, inverse, gain_two)
        gsum[rows, :] = grad_in
        low = grad_in.astype(BF16)
        g_low[rows, :] = low
        return (
            sums + jnp.sum(masked, axis=0, keepdims=True),
            gain_sum + jnp.sum(grad * normal, axis=0, keepdims=True),
            bias_sum + jnp.sum(grad, axis=0, keepdims=True),
            down_sum + jnp.sum(low.astype(F32), axis=0, keepdims=True),
        )

    sums, gain2, bias2, down_sum = lax.fori_loop(
        0, 4, norm_two, (zero_row, zero_row, zero_row, zero_row)
    )
    pool[sq] = jnp.broadcast_to(sums / count, (8, D))
    small[4:5, :] = down_sum
    small[10:11, :] = gain2
    small[11:12, :] = bias2

    out_moves = []
    for i, peer in enumerate(seq_peers):
        move = remote(
            bout.at[pl.ds(pl.multiple_of(peer * 128, 128), 128)], block_ref.at[sq, 0],
            out_send.at[0, i], out_recv.at[0, i], (dp, peer),
        )
        move.start()
        out_moves.append(move)
        move = remote(pool.at[sq], pool.at[sq], pool_send.at[i], pool_recv.at[i], (dp, peer))
        move.start()
        out_moves.append(move)
    own_b = pltpu.make_async_copy(bout.at[own_rows], block_ref.at[sq, 0], loc_sem.at[2])
    own_b.start()

    def add(left, right):
        return (left.astype(F32) + right.astype(F32)).astype(BF16)

    def piece(base, size):
        return pl.ds(pl.multiple_of(base, 16), size)

    gots = (got0, got1, got2, got3, got4)
    sums_of = (sum0, sum1, sum2, sum3)

    def double(spot_ref, rows, chunk, slots, send, recv):
        for e, peer in enumerate(w_peers):
            move = remote(spot_ref.at[chunk, rows], slots(e), send(e), recv(e), peer)
            move.start()
            move.wait()
            spot_ref[chunk, rows, :] = add(spot_ref[chunk, rows, :], slots(e)[...])

    def halve(n, order):
        chunk, first_row = n // 3, (n % 3) * 512
        stages = [halvings[name] for name in ("core",) + order]
        held, offset, base = part.at[chunk], first_row, first_row
        bases = []
        for level, (digit, peer) in enumerate(stages):
            size = 256 >> level
            move = remote(
                held.at[piece(offset + (1 - digit) * size, size)], gots[level].at[n],
                rs_send.at[level, n], rs_recv.at[level, n], peer,
            )
            move.start()
            yield
            move.wait()
            mine = held[piece(offset + digit * size, size), :]
            base = base + digit * size
            bases.append((base, size))
            if level < 4:
                sums_of[level][n] = add(mine, gots[level][n])
                held, offset = sums_of[level].at[n], 0
            else:
                full[chunk, piece(base, size), :] = add(mine, gots[level][n])
        double(
            full, piece(base, 16), chunk,
            lambda e: got4.at[6 + e * 6 + n],
            lambda e: rs_send.at[5 + e, n], lambda e: rs_recv.at[5 + e, n],
        )
        for level in (4, 3, 2, 1, 0):
            base, size = bases[level]
            spot = full.at[chunk, piece(base, size)]
            move = remote(spot, spot, ag_send.at[level, n], ag_recv.at[level, n], stages[level][1])
            move.start()
            yield
            move.wait()

    plane = 2 * yy + xx
    plane_peers = [(x_peer, yy * 2 + 1 - xx), (y_peer, (1 - yy) * 2 + xx), (xy_peer, (1 - yy) * 2 + 1 - xx)]

    def spread(b):
        rows = b * D
        move = remote(
            part.at[2, piece(rows + (1 - core) * 192, 192)], blk0.at[b],
            blk_send.at[0, b], blk_recv.at[0, b], core_peer,
        )
        move.start()
        yield
        move.wait()
        blk_sum[b] = add(part[2, piece(rows + core * 192, 192), :], blk0[b])
        moves = []
        for j, (peer, where) in enumerate(plane_peers):
            move = remote(
                blk_sum.at[b, piece(where * 48, 48)], blk1.at[b, j],
                blk_send.at[1 + j, b], blk_recv.at[1 + j, b], peer,
            )
            move.start()
            moves.append(move)
        yield
        total = blk_sum[b, piece(plane * 48, 48), :].astype(F32)
        for j in range(3):
            moves[j].wait()
            total = total + blk1[b, j].astype(F32)
        blk2[b, zz] = total.astype(BF16)
        moves = []
        for j, peer in enumerate(z_peers):
            move = remote(
                blk2.at[b, zz], blk2.at[b, zz], blk_send.at[4 + j, b], blk_recv.at[4 + j, b], peer,
            )
            move.start()
            moves.append(move)
        yield
        for move in moves:
            move.wait()
        mine = piece(rows + core * 192 + plane * 48, 48)
        full[2, mine, :] = (
            (blk2[b, 0].astype(F32) + blk2[b, 1].astype(F32))
            + (blk2[b, 2].astype(F32) + blk2[b, 3].astype(F32))
        ).astype(BF16)
        double(
            full, mine, 2,
            lambda e: blk2.at[b, 4 + e],
            lambda e: blk_send.at[11 + e, b], lambda e: blk_recv.at[11 + e, b],
        )
        moves = []
        for j, (peer, _) in enumerate(plane_peers):
            spot = full.at[2, mine]
            move = remote(spot, spot, blk_send.at[7 + j, b], blk_recv.at[7 + j, b], peer)
            move.start()
            moves.append(move)
        yield
        for move in moves:
            move.wait()
        spot = full.at[2, piece(rows + core * 192, 192)]
        move = remote(spot, spot, blk_send.at[10, b], blk_recv.at[10, b], core_peer)
        move.start()
        yield
        move.wait()

    def vectors():
        for step, peer in enumerate((core_peer, y_peer, x_peer)):
            move = remote(small, small_got.at[step], sm_send.at[step], sm_recv.at[step], peer)
            move.start()
            yield
            move.wait()
            small[...] = small[...] + small_got[step]
        small_z[zz] = small[...]
        moves = []
        for j, peer in enumerate(z_peers):
            move = remote(small_z.at[zz], small_z.at[zz], sm_send.at[3 + j], sm_recv.at[3 + j], peer)
            move.start()
            moves.append(move)
        yield
        for move in moves:
            move.wait()
        small[...] = (small_z[0] + small_z[1]) + (small_z[2] + small_z[3])
        for e, peer in enumerate(w_peers):
            move = remote(small, small_got.at[3 + e], sm_send.at[6 + e], sm_recv.at[6 + e], peer)
            move.start()
            move.wait()
            small[...] = small[...] + small_got[3 + e]

    agenda = []

    def launch(way, start, offsets):
        for i, offset in enumerate(offsets):
            agenda.append((start + offset, len(agenda), way))
        pump(start)

    def pump(now):
        agenda.sort(key=lambda entry: entry[:2])
        while agenda and agenda[0][0] <= now:
            _, _, way = agenda.pop(0)
            next(way, None)

    for i in range(3):
        part[0, i * 512 : (i + 1) * 512, :] = dot(
            active[:, i * 512 : (i + 1) * 512], g_low[...], TN
        ).astype(BF16)
        launch(halve(i, ORDERS[i]), 22.4 + 0.3 * i, HALVE_TIMES)

    def back_up(i, carry):
        cols = rows_of(i, 256)
        low = (dot(g_low[...], down_w[cols, :], NT) * slope[:, cols]).astype(BF16)
        g_up[:, cols] = low
        return carry

    lax.fori_loop(0, FF // 256, back_up, 0)
    pump(24.9)
    for i in range(4):
        small[i : i + 1, :] = jnp.sum(
            g_up[:, i * D : (i + 1) * D].astype(F32), axis=0, keepdims=True
        )
        part[1, i * D : (i + 1) * D, :] = dot(
            first_low[...], g_up[:, i * D : (i + 1) * D], TN
        ).astype(BF16)
    for i in range(3):
        launch(halve(3 + i, ORDERS[3 + i]), 25.6 + 0.1 * i, HALVE_TIMES)
    lower[...] = dot(g_up[...], up_w[...], NT)

    def norm_one_back(i, carry):
        gain_sum, bias_sum, out_sum = carry
        rows = rows_of(i, 128)
        grad = gsum[rows, :] + lower[rows, :]
        normal = y1[rows, :]
        grad_in = norm_back(grad, normal, r1[rows, :], gain_one)
        g_hid[rows, :] = grad_in
        low = grad_in.astype(BF16)
        g_low[rows, :] = low
        return (
            gain_sum + jnp.sum(grad * normal, axis=0, keepdims=True),
            bias_sum + jnp.sum(grad, axis=0, keepdims=True),
            out_sum + jnp.sum(low.astype(F32), axis=0, keepdims=True),
        )

    gain1, bias1, out_sum = lax.fori_loop(0, 4, norm_one_back, (zero_row, zero_row, zero_row))
    pump(26.6)
    small[5:6, :] = out_sum
    small[8:9, :] = gain1
    small[9:10, :] = bias1
    small[12:16, :] = jnp.zeros((4, D), F32)

    part[2, :D, :] = dot(c_t[...], g_low[...], NN).astype(BF16)
    launch(spread(0), 27.3, SPREAD_TIMES)
    gc_t[...] = dot(out_w[...], g_low[...], NT).astype(BF16)

    def attend_back(g, i):
        h = 4 * g + i
        rows = slice(h * HD, (h + 1) * HD)
        inverse = inv[h][:1, :]
        grad_c = (gc_t[rows, :].astype(F32) * inverse).astype(BF16)
        inner = jnp.sum(grad_c.astype(F32) * c_t[rows, :].astype(F32), axis=0, keepdims=True)
        grad_w = dot(v_x[h * VROWS : h * VROWS + HD, :], grad_c, TN)
        weights = probs[h]
        grad_s = (weights.astype(F32) * (grad_w - inner)).astype(BF16)
        base = g * D + i * HD
        gj_t[base : base + HD, :] = (dot(kz_t[rows, :], grad_s, NN) * SCALE).astype(BF16)
        gk = jnp.where(lane_valid, dot(q_t[rows, :], grad_s, NT) * SCALE, 0.0)
        gj_t[base + 128 : base + 128 + HD, :] = gk.astype(BF16)
        gv = jnp.where(lane_valid, dot(grad_c, weights, NT), 0.0)
        gj_t[base + 256 : base + 256 + HD, :] = gv.astype(BF16)

    clock = 27.6
    for g in range(GROUPS):
        for i in range(4):
            attend_back(g, i)
            clock += 0.67
            if i % 2 == 1:
                pump(clock)
        both = dot(x_t[...], gj_t[g * D : (g + 1) * D, :], NT)
        part[2, (g + 1) * D : (g + 2) * D, :] = both[:D, :].astype(BF16)
        small[6:7, g * 128 : (g + 1) * 128] = both[D : D + 1, :128]
        small[7:8, g * 128 : (g + 1) * 128] = both[D : D + 1, 256:]
        clock += 0.3
        launch(spread(g + 1), clock, SPREAD_TIMES)
    launch(vectors(), clock, VECTOR_TIMES)

    igr[...] = (g_hid[...] + dot(gj_t[...], qkv_t[...], TN)).astype(BF16)
    for i, peer in enumerate(seq_peers):
        move = remote(
            igr.at[pl.ds(pl.multiple_of(peer * 128, 128), 128)], igrad_ref.at[sq, 0],
            out_send.at[1, i], out_recv.at[1, i], (dp, peer),
        )
        move.start()
        out_moves.append(move)
    own_i = pltpu.make_async_copy(igr.at[own_rows], igrad_ref.at[sq, 0], loc_sem.at[3])
    own_i.start()

    pump(1e9)
    small_ref[...] = small[...]
    for move in out_moves:
        move.wait()
    pooled_ref[...] = pool[...]
    own_b.wait()
    own_i.wait()


def finish_kernel(
    grads_ref, small_ref, pool_ref, bl_ref, ig_ref,
    block_ref, pooled_ref, igrad_ref, qkv_ref, qb_ref, vb_ref, out_ref, ob_ref, g1_ref, b1_ref,
    up_ref, ub_ref, down_ref, db_ref, g2_ref, b2_ref,
    wide, out_sem, sem,
):
    moves = []
    for i, (src, dst) in enumerate(((bl_ref, block_ref), (ig_ref, igrad_ref))):
        move = pltpu.make_async_copy(src, dst, sem.at[i])
        move.start()
        moves.append(move)
    for i in range(4):
        ub_ref[i * D : (i + 1) * D] = small_ref[i, :]
    for m in range(4):
        pooled_ref[m] = pool_ref[m, :1, :]
    for row, ref in ((4, db_ref), (5, ob_ref), (6, qb_ref), (7, vb_ref), (8, g1_ref), (9, b1_ref), (10, g2_ref), (11, b2_ref)):
        ref[...] = small_ref[row, :]
    for i in range(12):
        wide[i] = grads_ref[i // 4, (i % 4) * D : (i % 4 + 1) * D, :].astype(F32)
        span = pl.ds((i % 4) * D, D)
        if i < 4:
            copies = [(wide.at[i], down_ref.at[span])]
        elif i < 8:
            copies = [(wide.at[i], up_ref.at[:, span])]
        elif i == 8:
            copies = [(wide.at[i], out_ref)]
        else:
            copies = [
                (wide.at[i, :, pl.ds(j * 128, 128)], qkv_ref.at[:, pl.ds(j * D + (i - 9) * 128, 128)])
                for j in range(3)
            ]
        for j, (src, dst) in enumerate(copies):
            move = pltpu.make_async_copy(src, dst, out_sem.at[i, j])
            move.start()
            moves.append(move)
    for move in moves:
        move.wait()


def body(
    ndp,
    inputs, lengths, cotangent, pool_cotangent, qkv_weight, query_bias, value_bias,
    out_weight, out_bias, norm1_gain, norm1_bias, up_weight, up_bias, down_weight,
    down_bias, norm2_gain, norm2_bias,
):
    any_spec = pl.BlockSpec(memory_space=pltpu.HBM)
    vmem = pl.BlockSpec(memory_space=pltpu.VMEM)
    smem = pl.BlockSpec(memory_space=pltpu.SMEM)
    extra = max(ndp.bit_length() - 4, 0)

    def v(*shape, dtype=BF16):
        return pltpu.VMEM(shape, dtype)

    dma = pltpu.SemaphoreType.DMA
    args = (
        inputs, lengths.T, cotangent, jnp.transpose(pool_cotangent, (1, 0, 2)),
        qkv_weight, query_bias, value_bias, out_weight, out_bias,
        norm1_gain, norm1_bias, up_weight, up_bias, down_weight, down_bias,
        norm2_gain, norm2_bias,
    )
    in_specs = [
        any_spec, smem, any_spec, vmem,
        any_spec, vmem, vmem, any_spec, vmem,
        vmem, vmem, any_spec, vmem, any_spec, vmem,
        vmem, vmem,
    ]
    results = pl.pallas_call(
        functools.partial(kernel, ndp),
        out_shape=(
            v(*inputs.shape), v(4, 8, D, dtype=F32), v(*inputs.shape), v(CHUNKS, ROWS, D), v(16, D, dtype=F32),
        ),
        in_specs=in_specs,
        out_specs=(vmem,) * 5,
        scratch_shapes=[
            v(512, D), v(512, D), v(D, 3 * D), v(D, D), v(D, FF), v(FF, D), v(3 * D, D), v(D + 16, 512),
            v(D, 512), v(D, 512), v(D, 512), v(H * VROWS, 512), v(H, 512, 512), v(H, 8, 512, dtype=F32),
            v(D, 512), v(512, D, dtype=F32), v(512, 1, dtype=F32), v(512, D), v(512, FF), v(512, FF, dtype=F32),
            v(512, D, dtype=F32), v(512, D, dtype=F32), v(512, D), v(512, FF), v(512, D, dtype=F32),
            v(D, 512), v(3 * D, 512), v(512, D), v(512, D), v(4, 8, D, dtype=F32),
            v(CHUNKS, ROWS, D), v(6, 256, D), v(6, 128, D), v(6, 64, D), v(6, 32, D), v(6 + 6 * extra, 16, D),
            v(6, 256, D), v(6, 128, D), v(6, 64, D), v(6, 32, D),
            v(4, 192, D), v(4, 3, 48, D), v(4, 4 + extra, 48, D), v(4, 192, D),
            v(16, D, dtype=F32), v(3 + extra, 16, D, dtype=F32), v(4, 16, D, dtype=F32), v(1, FF, dtype=F32),
            dma((4,)), dma((4,)), dma((2, 3)), dma((2, 3)), dma((2, 3)), dma((2, 3)), dma((3,)), dma((3,)),
            dma((5 + extra, 6)), dma((5 + extra, 6)), dma((5, 6)), dma((5, 6)),
            dma((11 + extra, 4)), dma((11 + extra, 4)), dma((6 + extra,)), dma((6 + extra,)),
        ],
        compiler_params=pltpu.CompilerParams(
            collective_id=0, has_side_effects=True, vmem_limit_bytes=56 * 2**20
        ),
    )(*args)
    block, pooled, igrad, grads, small = results

    def shape(*dims, dtype=F32):
        return jax.ShapeDtypeStruct(dims, dtype)

    outs = pl.pallas_call(
        finish_kernel,
        out_shape=(
            shape(*inputs.shape, dtype=BF16), shape(4, 1, D), shape(*inputs.shape, dtype=BF16),
            shape(D, 3 * D), shape(D), shape(D), shape(D, D), shape(D), shape(D), shape(D),
            shape(D, FF), shape(FF), shape(FF, D), shape(D), shape(D), shape(D),
        ),
        in_specs=[vmem] * 5,
        out_specs=(
            any_spec, vmem, any_spec, any_spec, vmem, vmem, any_spec, vmem, vmem, vmem,
            any_spec, vmem, any_spec, vmem, vmem, vmem,
        ),
        scratch_shapes=[v(12, D, D, dtype=F32), dma((12, 3)), dma((2,))],
        compiler_params=pltpu.CompilerParams(vmem_limit_bytes=24 * 2**20),
    )(grads, small, pooled, block, igrad)
    return outs


def solution(mesh):
    whole = P()
    return jax.shard_map(
        functools.partial(body, mesh.shape["dp"]),
        mesh=mesh,
        in_specs=(
            P(None, "dp", "seq", None), P(None, "dp"), P(None, "dp", "seq", None), P(None, "dp", None),
        ) + (whole,) * 13,
        out_specs=(
            P(None, "dp", "seq", None), P(None, "dp", None), P(None, "dp", "seq", None),
        ) + (whole,) * 13,
        check_vma=False,
    )
```

time: 115 us -> 83.4 us (0.73)
  Pallas kernels: 114 us -> 82.4 us
    pallas_call x1, Pallas kernels: 108 us -> 78.3 us  [body(): pl.pallas_call(functools.partial(kernel, ndp), out_shape=(v(*inputs.shape...]
    pallas_call x1, Pallas kernels: 5.83 us -> 4.12 us  [body(): pl.pallas_call(finish_kernel, out_shape=(shape(*inputs.shape, dtype=BF16)...]
where the time goes in v3:
time: 83.4 us; the launch traced here: 83.3 us
  Pallas kernels  82.4 us (99%)
    pallas_call x1, Pallas kernels, body(): pl.pallas_call(functools.partial(kernel, ndp), out_shape=(v(*inputs.shape...  78.3 us
    pallas_call x1, Pallas kernels, body(): pl.pallas_call(finish_kernel, out_shape=(shape(*inputs.shape, dtype=BF16)...  4.12 us

profile of v3, /device:TPU:0, one launch (start us, length us, event | category | flops | bytes accessed | tf_op | source)
XLA Modules:
  0.0 83.3 jit_solution(14102921851382017182)
XLA Ops:
  0.7 78.3 %shard_map.288 = (bf16[4,1,128,384]{3,2,1,0:T(8,128)(2,1)S(1)}, f32[4,8,384]{2,1,0:T(8,128)S(1)}, bf16[4,1,128,384]{3,2,1,0:T(8,128)(2,1)S(1)}, bf16[3,1536,384]{2,1,0:T(8,128)(2,1)S(1)}, f32[16,384]{1,0:T(8,128)S(1)}) custom-call(bf16[4,1,128,384]{3,2,1,0:T(8,128)(2,1)} %inputs_ref.1, s32[1,4]{1,0:T(1,128)} %bitcast.3, bf16[4,1,128,384]{3,2,1,0:T(8,128)(2,1)} %cot_ref.1, ...), custom_call_target="tpu_custom_call" | custom-call | tf_op jit(solution)/shard_map/pallas_call | solution.py:592
  79.0 4.1 %shard_map.289 = (bf16[4,1,128,384]{3,2,1,0:T(8,128)(2,1)}, f32[4,1,384]{2,1,0:T(1,128)}, bf16[4,1,128,384]{3,2,1,0:T(8,128)(2,1)}, f32[384,1152]{1,0:T(8,128)},...) custom-call(bf16[3,1536,384]{2,1,0:T(8,128)(2,1)S(1)} %get-tuple-ele, ...), custom_call_target="tpu_custom_call" | custom-call | tf_op jit(solution)/shard_map/pallas_call | solution.py:622

commit v4 on v3

v4 whole, which is shorter than its diff:
```python
import functools

import jax
import jax.numpy as jnp
from jax import lax
from jax.experimental import pallas as pl
from jax.experimental.pallas import tpu as pltpu
from jax.sharding import PartitionSpec as P

H = 12
HD = 32
D = 384
FF = 1536
EPS = 1e-6
F32 = jnp.float32
BF16 = jnp.bfloat16
MESH = pl.DeviceIdType.MESH
NN = (((1,), (0,)), ((), ()))
NT = (((1,), (1,)), ((), ()))
TN = (((0,), (0,)), ((), ()))
LOG2E = 1.4426950408889634
SCALE = HD**-0.5
VROWS = HD + 16
CHUNKS = 3
ROWS = 1536
GROUPS = 3
PLAN = (
    (0, 512, ("core", "z1", "xy", "z2")),
    (512, 512, ("core", "z1", "z2", "xy")),
    (1024, 512, ("core", "xy", "z")),
    (1536, 512, ("core", "z1", "xy", "z2")),
    (2048, 512, ("core", "x", "y", "z")),
    (2560, 512, ("core", "z", "x", "y")),
    (3072, 512, ("core", "xy", "z")),
    (3584, 384, ("core", "xy", "all_z")),
    (3968, 384, ("core", "xy", "all_z")),
    (4352, 256, ("core", "xy", "all_z")),
)
SCHEDULE = (
    -1, -1, -1, 0, 1, -1, 2, -1, -1, -1, -1, 3, 4, 5, 0, -1, 10, -1, 1, 2, -1, -1, -1, 4, 3, 6, -1, 0,
    -1, 10, -1, -1, 5, 4, 1, 7, -1, 3, -1, 0, 2, -1, 6, 5, 8, -1, 1, 10, 4, -1, 3, -1, 7, 5, 9, 0, 11,
    2, 8, 6, 1, 5, 4, 3, 9, 12, 0, 11, 7, 5, 2, 4, 2, 8, 3, 6, 1, 0, 4, 0, 9, 4, 7, 11, 7, 8, 3, 8, 6,
    3, 5, 9, 1, 6, 5, 9, 1,
)


def dot(left, right, dims):
    return lax.dot_general(left, right, dims, preferred_element_type=F32)


def gelu_and_slope(upper):
    cdf = 0.5 * (1.0 + lax.erf(upper * 2.0**-0.5))
    density = jnp.exp2((-0.5 * LOG2E) * (upper * upper)) * (2.0 * jnp.pi) ** -0.5
    return upper * cdf, cdf + upper * density


def layer_norm(values):
    centre = values - jnp.mean(values, axis=-1, keepdims=True)
    inverse = lax.rsqrt(jnp.mean(centre * centre, axis=-1, keepdims=True) + EPS)
    return centre * inverse, inverse


def norm_back(grad_out, normal, inverse, gain):
    scaled = grad_out * gain
    return inverse * (
        scaled
        - jnp.mean(scaled, axis=-1, keepdims=True)
        - normal * jnp.mean(scaled * normal, axis=-1, keepdims=True)
    )


def kernel(
    ndp,
    inputs_ref, lengths_ref, cot_ref, pool_ref,
    qkv_hbm, qb_ref, vb_ref, out_hbm, ob_ref, g1_ref, b1_ref,
    up_hbm, ub_ref, down_hbm, db_ref, g2_ref, b2_ref,
    block_ref, pooled_ref, igrad_ref, full, small_ref,
    x, cot, qkv_w, out_w, up_w, down_w, qkv_t,
    q_t, kd_t, kz_t, v_x, probs, inv, c_t, y1, r1, first_low, active, slope,
    lower, gsum, g_low, g_up, g_hid, gc_t, gj_t, bout, igr, pool,
    part, small, late, up_row,
    w_sem, loc_sem, in_send, in_recv, out_send, out_recv, pool_send, pool_recv,
    s_a, s_b, gs_t, gs_n, p_n, *travel_refs,
):
    dp = lax.axis_index("dp")
    sq = lax.axis_index("seq")
    core = lax.rem(sq, 2)
    yy = lax.div(sq, 2)
    xx = lax.rem(dp, 2)
    zz = lax.rem(lax.div(dp, 2), 4)
    extra = []
    bit = 8
    while bit < ndp:
        extra.append(bit)
        bit *= 2

    def flip(index, amount):
        digit = lax.rem(lax.div(index, amount), 2)
        return index + amount * (1 - 2 * digit)

    seq_peers = [lax.rem(sq + step, 4) for step in (1, 2, 3)]
    core_peer = (dp, flip(sq, 1))
    y_peer = (dp, flip(sq, 2))
    x_peer = (flip(dp, 1), sq)
    xy_peer = (flip(dp, 1), flip(sq, 2))
    z_peers = [(dp + 2 * (lax.rem(zz + step, 4) - zz), sq) for step in (1, 2, 3)]
    w_peers = [(flip(dp, amount), sq) for amount in extra]
    greeted = [(dp, peer) for peer in seq_peers] + [x_peer, xy_peer] + z_peers + w_peers
    halvings = {
        "core": (core, core_peer),
        "y": (yy, y_peer),
        "x": (xx, x_peer),
        "z1": (lax.rem(zz, 2), (flip(dp, 2), sq)),
        "z2": (lax.div(zz, 2), (flip(dp, 4), sq)),
    }

    loads = [
        pltpu.make_async_copy(src, dst, w_sem.at[i])
        for i, (src, dst) in enumerate(
            [(qkv_hbm, qkv_w), (out_hbm, out_w), (up_hbm, up_w), (down_hbm, down_w)]
        )
    ]
    for load in loads:
        load.start()
    own_rows = pl.ds(pl.multiple_of(sq * 128, 128), 128)
    own_x = pltpu.make_async_copy(inputs_ref.at[sq, 0], x.at[own_rows], loc_sem.at[0])
    own_c = pltpu.make_async_copy(cot_ref.at[sq, 0], cot.at[own_rows], loc_sem.at[1])
    own_x.start()
    own_c.start()

    barrier = pltpu.get_barrier_semaphore()
    for peer in greeted:
        pl.semaphore_signal(barrier, inc=1, device_id=peer, device_id_type=MESH)
    pl.semaphore_wait(barrier, len(greeted))

    def remote(src, dst, send, recv, peer):
        return pltpu.make_async_remote_copy(
            src_ref=src, dst_ref=dst, send_sem=send, recv_sem=recv,
            device_id=peer, device_id_type=MESH,
        )

    x_moves, c_moves = [], []
    for which, (src, dst, moves) in enumerate(((inputs_ref, x, x_moves), (cot_ref, cot, c_moves))):
        for i, peer in enumerate(seq_peers):
            move = remote(
                src.at[peer, 0], dst.at[own_rows],
                in_send.at[which, i], in_recv.at[which, i], (dp, peer),
            )
            moves.append(move)
    for move in x_moves:
        move.start()

    span = lengths_ref[0, sq]
    query_bias, value_bias, out_bias, gain_one, bias_one, up_bias, down_bias, gain_two, bias_two = (
        ref[...].reshape(1, -1)
        for ref in (qb_ref, vb_ref, ob_ref, g1_ref, b1_ref, ub_ref, db_ref, g2_ref, b2_ref)
    )
    up_row[...] = up_bias
    count = span.astype(F32)
    lane_valid = lax.broadcasted_iota(jnp.int32, (1, 512), 1) < span

    loads[0].wait()

    for i in range(3):
        for g in range(GROUPS):
            turned = qkv_w[:, i * D + g * 128 : i * D + (g + 1) * 128].T
            for j in range(2):
                first = (2 * g + j) * 192 + i * 64
                qkv_t[first : first + 64, :] = turned[j * 64 : (j + 1) * 64]
    own_x.wait()
    for move in x_moves:
        move.wait()
    for move in c_moves:
        move.start()

    qcol = jnp.broadcast_to(query_bias, (8, D)).T[:, :1]
    vcol = jnp.broadcast_to(value_bias, (8, D)).T[:, :1]
    ones_row = jnp.broadcast_to(jnp.where(lane_valid, 1.0, 0.0), (16, 512)).astype(BF16)
    for g in range(GROUPS):
        joined = dot(qkv_t[g * D : (g + 1) * D, :], x[...], NT)
        for j in range(2):
            feats = slice((2 * g + j) * 64, (2 * g + j + 1) * 64)
            first = j * 192
            q_t[feats, :] = (joined[first : first + 64] + qcol[feats]).astype(BF16)
            keys = joined[first + 64 : first + 128]
            kd_t[feats, :] = jnp.where(lane_valid, keys, keys[:, :1]).astype(BF16)
            kz_t[feats, :] = jnp.where(lane_valid, keys, 0.0).astype(BF16)
            values = jnp.where(lane_valid, joined[first + 128 : first + 192] + vcol[feats], 0.0).astype(BF16)
            for i in range(2):
                h = 4 * g + 2 * j + i
                v_x[h * VROWS : h * VROWS + HD, :] = values[i * HD : (i + 1) * HD, :]
                v_x[h * VROWS + HD : (h + 1) * VROWS, :] = ones_row

    def score(h):
        rows = slice(h * HD, (h + 1) * HD)
        return dot(kd_t[rows, :], q_t[rows, :], TN)

    def soften(scores):
        peak = jnp.max(scores, axis=0, keepdims=True)
        return jnp.exp2(scores * (SCALE * LOG2E) - peak * (SCALE * LOG2E)).astype(BF16)

    def gather(h, raised):
        both = dot(v_x[h * VROWS : (h + 1) * VROWS, :], raised, NN)
        inverse = 1.0 / both[HD : HD + 1, :]
        inv[h] = jnp.broadcast_to(inverse, (8, 512))
        c_t[h * HD : (h + 1) * HD, :] = (both[:HD, :] * inverse).astype(BF16)

    sbufs = (s_a, s_b)
    s_a[...] = score(0)
    for h in range(H):
        if h + 1 < H:
            sbufs[(h + 1) % 2][...] = score(h + 1)
        for q in range(4):
            probs[h, :, q * 128 : (q + 1) * 128] = soften(sbufs[h % 2][:, q * 128 : (q + 1) * 128])
        gather(h, probs[h])

    loads[1].wait()

    lower[...] = dot(c_t[...], out_w[...], TN)

    def norm_one(i):
        rows = slice(i * 128, (i + 1) * 128)
        normal, inverse = layer_norm(x[rows, :].astype(F32) + lower[rows, :] + out_bias)
        y1[rows, :] = normal
        r1[rows, :] = inverse
        first_low[rows, :] = (normal * gain_one + bias_one).astype(BF16)

    for i in range(4):
        norm_one(i)
    loads[2].wait()

    def raise_up(i):
        cols = slice(i * 256, (i + 1) * 256)
        upper = dot(first_low[...], up_w[:, cols], NN) + up_row[:, cols]
        act, slp = gelu_and_slope(upper)
        active[:, cols] = act.astype(BF16)
        slope[:, cols] = slp

    for i in range(FF // 256):
        raise_up(i)
    loads[3].wait()
    lower[...] = dot(active[...], down_w[...], NN)
    own_c.wait()
    for move in c_moves:
        move.wait()
    chosen = lax.broadcasted_iota(jnp.int32, (4, D), 0) == sq
    pool_share = jnp.sum(jnp.where(chosen, pool_ref[0].astype(F32), 0.0), axis=0, keepdims=True) / count

    zero_row = jnp.zeros((1, D), F32)

    def norm_two(i, carry):
        sums, gain_sum, bias_sum, down_sum = carry
        rows = slice(i * 128, (i + 1) * 128)
        firsts = y1[rows, :] * gain_one + bias_one
        normal, inverse = layer_norm(firsts + lower[rows, :] + down_bias)
        here = lax.broadcasted_iota(jnp.int32, (128, 1), 0) + i * 128 < span
        masked = jnp.where(here, normal * gain_two + bias_two, 0.0)
        bout[rows, :] = masked.astype(BF16)
        grad = jnp.where(here, cot[rows, :].astype(F32) + pool_share, 0.0)
        grad_in = norm_back(grad, normal, inverse, gain_two)
        gsum[rows, :] = grad_in
        low = grad_in.astype(BF16)
        g_low[rows, :] = low
        return (
            sums + jnp.sum(masked, axis=0, keepdims=True),
            gain_sum + jnp.sum(grad * normal, axis=0, keepdims=True),
            bias_sum + jnp.sum(grad, axis=0, keepdims=True),
            down_sum + jnp.sum(low.astype(F32), axis=0, keepdims=True),
        )

    carry = (zero_row, zero_row, zero_row, zero_row)
    for i in range(4):
        carry = norm_two(i, carry)
    sums, gain2, bias2, down_sum = carry
    pool[sq] = jnp.broadcast_to(sums / count, (8, D))
    small[4:5, :] = down_sum
    small[10:11, :] = gain2
    small[11:12, :] = bias2

    out_moves = []
    for i, peer in enumerate(seq_peers):
        move = remote(
            bout.at[pl.ds(pl.multiple_of(peer * 128, 128), 128)], block_ref.at[sq, 0],
            out_send.at[0, i], out_recv.at[0, i], (dp, peer),
        )
        move.start()
        out_moves.append(move)
        move = remote(pool.at[sq], pool.at[sq], pool_send.at[i], pool_recv.at[i], (dp, peer))
        move.start()
        out_moves.append(move)
    own_b = pltpu.make_async_copy(bout.at[own_rows], block_ref.at[sq, 0], loc_sem.at[2])
    own_b.start()

    def add(left, right):
        return (left.astype(F32) + right.astype(F32)).astype(BF16)

    def piece(base, size):
        return pl.ds(base if isinstance(base, int) else pl.multiple_of(base, 16), size)

    plane = 2 * yy + xx
    plane_peers = [(x_peer, yy * 2 + 1 - xx), (y_peer, (1 - yy) * 2 + xx), (xy_peer, (1 - yy) * 2 + 1 - xx)]
    z_places = [(peer, lax.rem(zz + 1 + j, 4)) for j, peer in enumerate(z_peers)]
    groups = {name: (digit, [(peer, 1 - digit)]) for name, (digit, peer) in halvings.items()}
    groups["xy"] = (plane, plane_peers)
    groups["z"] = groups["all_z"] = (zz, z_places)
    refs = list(travel_refs)

    def travel(first, rows, way):
        levels = len(way)
        gots = [refs.pop(0) for _ in range(levels)]
        sums = [refs.pop(0) for _ in range(levels - 1)]
        more = refs.pop(0) if w_peers else None
        send, recv = refs.pop(0), refs.pop(0)
        return steps_of(first, rows, way, gots, sums, more, send, recv)

    def steps_of(first, rows, way, gots, sums, more, send, recv):
        used = iter(range(100))
        held, offset, base, size = part, first, first, rows
        places = []
        for level, name in enumerate(way):
            index, peers = groups[name]
            moves = []
            if name == "all_z":
                gots[level][index] = held[piece(offset, size), :]
                mine = gots[level].at[index]
                for peer, _ in peers:
                    n = next(used)
                    moves.append(remote(mine, mine, send.at[n], recv.at[n], peer))
            else:
                size //= len(peers) + 1
                for j, (peer, where) in enumerate(peers):
                    n = next(used)
                    moves.append(remote(
                        held.at[piece(offset + where * size, size)], gots[level].at[j],
                        send.at[n], recv.at[n], peer,
                    ))
            for move in moves:
                move.start()
            yield
            for move in moves:
                move.wait()
            if name == "all_z":
                terms = [gots[level][j].astype(F32) for j in range(4)]
                total = (terms[0] + terms[1]) + (terms[2] + terms[3])
            else:
                total = held[piece(offset + index * size, size), :].astype(F32)
                for j in range(len(peers)):
                    total = total + gots[level][j].astype(F32)
                base = base + index * size
                places.append((base, size, peers))
            if level < len(way) - 1:
                sums[level][...] = total.astype(BF16)
                held, offset = sums[level], 0
            else:
                full[piece(base, size), :] = total.astype(BF16)
        for e, peer in enumerate(w_peers):
            n = next(used)
            spot = full.at[piece(base, size)]
            move = remote(spot, more.at[e], send.at[n], recv.at[n], peer)
            move.start()
            move.wait()
            full[piece(base, size), :] = add(full[piece(base, size), :], more[e])
        for base, size, peers in reversed(places):
            moves = []
            for peer, _ in peers:
                n = next(used)
                spot = full.at[piece(base, size)]
                moves.append(remote(spot, spot, send.at[n], recv.at[n], peer))
            for move in moves:
                move.start()
            yield
            for move in moves:
                move.wait()

    def vectors(mine, got, planes, zs, more, send, recv):
        move = remote(mine, got, send.at[0], recv.at[0], core_peer)
        move.start()
        yield
        move.wait()
        total = mine[...] + got[...]
        for slots, index, peers, n in ((planes, plane, plane_peers, 1), (zs, zz, z_places, 4)):
            slots[index] = total
            moves = [
                remote(slots.at[index], slots.at[index], send.at[n + j], recv.at[n + j], peer)
                for j, (peer, _) in enumerate(peers)
            ]
            for move in moves:
                move.start()
            yield
            for move in moves:
                move.wait()
            total = (slots[0] + slots[1]) + (slots[2] + slots[3])
        mine[...] = total
        for e, peer in enumerate(w_peers):
            move = remote(mine, more.at[e], send.at[7 + e], recv.at[7 + e], peer)
            move.start()
            move.wait()
            mine[...] = mine[...] + more[e]

    def back_home():
        for i, peer in enumerate(seq_peers):
            move = remote(
                igr.at[pl.ds(pl.multiple_of(peer * 128, 128), 128)], igrad_ref.at[sq, 0],
                out_send.at[1, i], out_recv.at[1, i], (dp, peer),
            )
            move.start()
            out_moves.append(move)
        yield

    def vector_refs():
        got, planes, zs = refs.pop(0), refs.pop(0), refs.pop(0)
        more = refs.pop(0) if w_peers else None
        return got, planes, zs, more, refs.pop(0), refs.pop(0)

    travels = [travel(*entry) for entry in PLAN]
    travels += [vectors(small, *vector_refs()), vectors(late, *vector_refs()), back_home()]
    agenda = list(SCHEDULE)

    def go():
        while agenda and agenda[0] >= 0:
            next(travels[agenda.pop(0)], None)
        if agenda:
            agenda.pop(0)

    def launch(n):
        next(travels[n])

    for i in range(3):
        part[i * 512 : (i + 1) * 512, :] = dot(
            active[:, i * 512 : (i + 1) * 512], g_low[...], TN
        ).astype(BF16)
        launch(i)
        go()

    for j in range(3):
        for i in (2 * j, 2 * j + 1):
            cols = slice(i * 256, (i + 1) * 256)
            g_up[:, cols] = (dot(g_low[...], down_w[cols, :], NT) * slope[:, cols]).astype(BF16)
        go()
    for i in range(4):
        small[i : i + 1, :] = jnp.sum(
            g_up[:, i * D : (i + 1) * D].astype(F32), axis=0, keepdims=True
        )
        part[ROWS + i * D : ROWS + (i + 1) * D, :] = dot(
            first_low[...], g_up[:, i * D : (i + 1) * D], TN
        ).astype(BF16)
    for i in range(3):
        launch(3 + i)
    go()
    lower[...] = dot(g_up[...], up_w[...], NT)
    go()

    def norm_one_back(i, carry):
        gain_sum, bias_sum, out_sum = carry
        rows = slice(i * 128, (i + 1) * 128)
        grad = gsum[rows, :] + lower[rows, :]
        normal = y1[rows, :]
        grad_in = norm_back(grad, normal, r1[rows, :], gain_one)
        g_hid[rows, :] = grad_in
        low = grad_in.astype(BF16)
        g_low[rows, :] = low
        return (
            gain_sum + jnp.sum(grad * normal, axis=0, keepdims=True),
            bias_sum + jnp.sum(grad, axis=0, keepdims=True),
            out_sum + jnp.sum(low.astype(F32), axis=0, keepdims=True),
        )

    carry = (zero_row, zero_row, zero_row)
    for i in range(4):
        carry = norm_one_back(i, carry)
    gain1, bias1, out_sum = carry
    small[5:6, :] = out_sum
    small[8:9, :] = gain1
    small[9:10, :] = bias1
    small[6:8, :] = jnp.zeros((2, D), F32)
    small[12:16, :] = jnp.zeros((4, D), F32)
    launch(len(PLAN))
    go()

    part[2 * ROWS : 2 * ROWS + D, :] = dot(c_t[...], g_low[...], NN).astype(BF16)
    gc_t[...] = dot(out_w[...], g_low[...], NT).astype(BF16)
    go()

    def scale_c(h):
        rows = slice(h * HD, (h + 1) * HD)
        return (gc_t[rows, :].astype(F32) * inv[h][:1, :]).astype(BF16)

    def grad_weights(h):
        sbufs[h % 2][...] = dot(v_x[h * VROWS : h * VROWS + HD, :], scale_c(h), TN)

    grad_weights(0)

    def attend_back(h):
        rows = slice(h * HD, (h + 1) * HD)
        if h + 1 < H:
            grad_weights(h + 1)
        grad_c = scale_c(h)
        inner = jnp.sum(grad_c.astype(F32) * c_t[rows, :].astype(F32), axis=0, keepdims=True)
        weights = probs[h]
        gs_t[...] = (weights.astype(F32) * (sbufs[h % 2][...] - inner)).astype(BF16)
        gs_n[...] = gs_t[...].T
        p_n[...] = weights.T
        base = (h // 2) * 192 + (h % 2) * HD
        gv = jnp.where(lane_valid, dot(grad_c, p_n[...], NN), 0.0)
        gj_t[base + 128 : base + 128 + HD, :] = gv.astype(BF16)
        gj_t[base : base + HD, :] = (dot(kz_t[rows, :], gs_t[...], NN) * SCALE).astype(BF16)
        gk = jnp.where(lane_valid, dot(q_t[rows, :], gs_n[...], NN) * SCALE, 0.0)
        gj_t[base + 64 : base + 64 + HD, :] = gk.astype(BF16)

    for h in range(H):
        attend_back(h)
        if h % 2 == 1:
            first = (h // 2) * 192
            begin = 2 * ROWS + D + first
            part[begin : begin + 192, :] = dot(gj_t[first : first + 192, :], x[...], NN).astype(BF16)
            ready = begin + 192
            for n in range(6, len(PLAN)):
                if ready - 192 < PLAN[n][0] + PLAN[n][1] <= ready:
                    launch(n)
        go()
    query_sums, value_sums = [], []
    for g in range(H // 2):
        both = dot(jnp.ones((16, 512), BF16), gj_t[g * 192 : (g + 1) * 192, :], NT)
        query_sums.append(both[:1, :64])
        value_sums.append(both[:1, 128:])
    late[...] = jnp.concatenate(
        [
            jnp.concatenate(query_sums, axis=1),
            jnp.concatenate(value_sums, axis=1),
            jnp.zeros((6, D), F32),
        ],
        axis=0,
    )
    launch(len(PLAN) + 1)
    go()

    igr[...] = (g_hid[...] + dot(gj_t[...], qkv_t[...], TN)).astype(BF16)
    own_i = pltpu.make_async_copy(igr.at[own_rows], igrad_ref.at[sq, 0], loc_sem.at[3])
    own_i.start()
    go()

    go()
    small_ref[...] = small[...]
    small_ref[6:8, :] = late[:2, :]
    for move in out_moves:
        move.wait()
    pooled_ref[...] = pool[...]
    own_b.wait()
    own_i.wait()


def finish_kernel(
    grads_ref, small_ref, pool_ref, bl_ref, ig_ref,
    block_ref, pooled_ref, igrad_ref, qkv_ref, qb_ref, vb_ref, out_ref, ob_ref, g1_ref, b1_ref,
    up_ref, ub_ref, down_ref, db_ref, g2_ref, b2_ref,
    wide, out_sem, sem,
):
    moves = []
    for i, (src, dst) in enumerate(((bl_ref, block_ref), (ig_ref, igrad_ref))):
        move = pltpu.make_async_copy(src, dst, sem.at[i])
        move.start()
        moves.append(move)
    for i in range(4):
        ub_ref[i * D : (i + 1) * D] = small_ref[i, :]
    for m in range(4):
        pooled_ref[m] = pool_ref[m, :1, :]
    for row, ref in ((4, db_ref), (5, ob_ref), (6, qb_ref), (7, vb_ref), (8, g1_ref), (9, b1_ref), (10, g2_ref), (11, b2_ref)):
        ref[...] = small_ref[row, :]
    for i in range(12):
        if i < 9:
            wide[i] = grads_ref[i * D : (i + 1) * D, :].astype(F32)
        else:
            first = 9 * D + (i - 9) * 64
            turned = [grads_ref[first + g * 192 : first + g * 192 + 64, :] for g in range(H // 2)]
            wide[i] = jnp.concatenate(turned, axis=0).T.astype(F32)
        span = pl.ds((i % 4) * D, D)
        if i < 4:
            copies = [(wide.at[i], down_ref.at[span])]
        elif i < 8:
            copies = [(wide.at[i], up_ref.at[:, span])]
        elif i == 8:
            copies = [(wide.at[i], out_ref)]
        else:
            copies = [(wide.at[i], qkv_ref.at[:, pl.ds((i - 9) * D, D)])]
        for j, (src, dst) in enumerate(copies):
            move = pltpu.make_async_copy(src, dst, out_sem.at[i, j])
            move.start()
            moves.append(move)
    for move in moves:
        move.wait()


def travel_scratch(rows, way, extra):
    gots, sums, count = [], [], extra
    for name in way:
        peers = {"xy": 3, "z": 3, "all_z": 3}.get(name, 1)
        if name == "all_z":
            gots.append(pltpu.VMEM((4, rows, D), BF16))
            count += 3
        else:
            rows //= peers + 1
            gots.append(pltpu.VMEM((peers, rows, D), BF16))
            count += 2 * peers
        sums.append(pltpu.VMEM((rows, D), BF16))
    more = [pltpu.VMEM((extra, rows, D), BF16)] if extra else []
    return gots + sums[:-1] + more + [pltpu.SemaphoreType.DMA((count,))] * 2


def vector_scratch(rows, extra):
    slots = [pltpu.VMEM((rows, D), F32), pltpu.VMEM((4, rows, D), F32), pltpu.VMEM((4, rows, D), F32)]
    more = [pltpu.VMEM((extra, rows, D), F32)] if extra else []
    return slots + more + [pltpu.SemaphoreType.DMA((7 + extra,))] * 2


def body(
    ndp,
    inputs, lengths, cotangent, pool_cotangent, qkv_weight, query_bias, value_bias,
    out_weight, out_bias, norm1_gain, norm1_bias, up_weight, up_bias, down_weight,
    down_bias, norm2_gain, norm2_bias,
):
    any_spec = pl.BlockSpec(memory_space=pltpu.HBM)
    vmem = pl.BlockSpec(memory_space=pltpu.VMEM)
    smem = pl.BlockSpec(memory_space=pltpu.SMEM)
    extra = max(ndp.bit_length() - 4, 0)

    def v(*shape, dtype=BF16):
        return pltpu.VMEM(shape, dtype)

    dma = pltpu.SemaphoreType.DMA
    args = (
        inputs, lengths.T, cotangent, jnp.transpose(pool_cotangent, (1, 0, 2)),
        qkv_weight, query_bias, value_bias, out_weight, out_bias,
        norm1_gain, norm1_bias, up_weight, up_bias, down_weight, down_bias,
        norm2_gain, norm2_bias,
    )
    in_specs = [
        any_spec, smem, any_spec, vmem,
        any_spec, vmem, vmem, any_spec, vmem,
        vmem, vmem, any_spec, vmem, any_spec, vmem,
        vmem, vmem,
    ]
    results = pl.pallas_call(
        functools.partial(kernel, ndp),
        out_shape=(
            v(*inputs.shape), v(4, 8, D, dtype=F32), v(*inputs.shape), v(CHUNKS * ROWS, D), v(16, D, dtype=F32),
        ),
        in_specs=in_specs,
        out_specs=(vmem,) * 5,
        scratch_shapes=[
            v(512, D), v(512, D), v(D, 3 * D), v(D, D), v(D, FF), v(FF, D), v(3 * D, D),
            v(D, 512), v(D, 512), v(D, 512), v(H * VROWS, 512), v(H, 512, 512), v(H, 8, 512, dtype=F32),
            v(D, 512), v(512, D, dtype=F32), v(512, 1, dtype=F32), v(512, D), v(512, FF), v(512, FF, dtype=F32),
            v(512, D, dtype=F32), v(512, D, dtype=F32), v(512, D), v(512, FF), v(512, D, dtype=F32),
            v(D, 512), v(3 * D, 512), v(512, D), v(512, D), v(4, 8, D, dtype=F32),
            v(CHUNKS * ROWS, D),
            v(16, D, dtype=F32), v(8, D, dtype=F32), v(1, FF, dtype=F32),
            dma((4,)), dma((4,)), dma((2, 3)), dma((2, 3)), dma((2, 3)), dma((2, 3)), dma((3,)), dma((3,)),
            v(512, 512, dtype=F32), v(512, 512, dtype=F32), v(512, 512), v(512, 512), v(512, 512),
            *[item for _, rows, way in PLAN for item in travel_scratch(rows, way, extra)],
            *[item for rows in (16, 8) for item in vector_scratch(rows, extra)],
        ],
        compiler_params=pltpu.CompilerParams(
            collective_id=0, has_side_effects=True, vmem_limit_bytes=56 * 2**20
        ),
    )(*args)
    block, pooled, igrad, grads, small = results

    def shape(*dims, dtype=F32):
        return jax.ShapeDtypeStruct(dims, dtype)

    outs = pl.pallas_call(
        finish_kernel,
        out_shape=(
            shape(*inputs.shape, dtype=BF16), shape(4, 1, D), shape(*inputs.shape, dtype=BF16),
            shape(D, 3 * D), shape(D), shape(D), shape(D, D), shape(D), shape(D), shape(D),
            shape(D, FF), shape(FF), shape(FF, D), shape(D), shape(D), shape(D),
        ),
        in_specs=[vmem] * 5,
        out_specs=(
            any_spec, vmem, any_spec, any_spec, vmem, vmem, any_spec, vmem, vmem, vmem,
            any_spec, vmem, any_spec, vmem, vmem, vmem,
        ),
        scratch_shapes=[v(12, D, D, dtype=F32), dma((12, 3)), dma((2,))],
        compiler_params=pltpu.CompilerParams(vmem_limit_bytes=24 * 2**20),
    )(grads, small, pooled, block, igrad)
    return outs


def solution(mesh):
    whole = P()
    return jax.shard_map(
        functools.partial(body, mesh.shape["dp"]),
        mesh=mesh,
        in_specs=(
            P(None, "dp", "seq", None), P(None, "dp"), P(None, "dp", "seq", None), P(None, "dp", None),
        ) + (whole,) * 13,
        out_specs=(
            P(None, "dp", "seq", None), P(None, "dp", None), P(None, "dp", "seq", None),
        ) + (whole,) * 13,
        check_vma=False,
    )
```

time: 83.4 us -> 74.2 us (0.89)
  Pallas kernels: 82.4 us -> 73.2 us
    pallas_call x1, Pallas kernels: 78.3 us -> 69 us  [body(): pl.pallas_call(functools.partial(kernel, ndp), out_shape=(v(*inputs.shape...]
where the time goes in v4:
time: 74.2 us; the launch traced here: 74 us
  Pallas kernels  73.2 us (99%)
  between operations  0.82 us (1%)
    pallas_call x1, Pallas kernels, body(): pl.pallas_call(functools.partial(kernel, ndp), out_shape=(v(*inputs.shape...  69 us
    pallas_call x1, Pallas kernels, body(): pl.pallas_call(finish_kernel, out_shape=(shape(*inputs.shape, dtype=BF16)...  4.16 us

profile of v4, /device:TPU:0, one launch (start us, length us, event | category | flops | bytes accessed | tf_op | source)
XLA Modules:
  0.0 74.0 jit_solution(11924539896829399366)
XLA Ops:
  0.7 69.0 %shard_map.288 = (bf16[4,1,128,384]{3,2,1,0:T(8,128)(2,1)S(1)}, f32[4,8,384]{2,1,0:T(8,128)S(1)}, bf16[4,1,128,384]{3,2,1,0:T(8,128)(2,1)S(1)}, bf16[4608,384]{1,0:T(8,128)(2,1)S(1)}, f32[16,384]{1,0:T(8,128)S(1)}) custom-call(bf16[4,1,128,384]{3,2,1,0:T(8,128)(2,1)} %inputs_ref.1, s32[1,4]{1,0:T(1,128)} %bitcast.3, bf16[4,1,128,384]{3,2,1,0:T(8,128)(2,1)} %cot_ref.1, ...), custom_call_target="tpu_custom_call" | custom-call | tf_op jit(solution)/shard_map/pallas_call | solution.py:642
  69.7 4.2 %shard_map.289 = (bf16[4,1,128,384]{3,2,1,0:T(8,128)(2,1)}, f32[4,1,384]{2,1,0:T(1,128)}, bf16[4,1,128,384]{3,2,1,0:T(8,128)(2,1)}, f32[384,1152]{1,0:T(8,128)},...) custom-call(bf16[4608,384]{1,0:T(8,128)(2,1)S(1)} %get-tuple-element, ...), custom_call_target="tpu_custom_call" | custom-call | tf_op jit(solution)/shard_map/pallas_call | solution.py:671

commit v5 on v4

--- a/solution.py
+++ b/solution.py
@@ -24,23 +24,26 @@
 CHUNKS = 3
 ROWS = 1536
 GROUPS = 3
+WIDE = 2 * ROWS + D
 PLAN = (
-    (0, 512, ("core", "z1", "xy", "z2")),
-    (512, 512, ("core", "z1", "z2", "xy")),
-    (1024, 512, ("core", "xy", "z")),
-    (1536, 512, ("core", "z1", "xy", "z2")),
-    (2048, 512, ("core", "x", "y", "z")),
-    (2560, 512, ("core", "z", "x", "y")),
-    (3072, 512, ("core", "xy", "z")),
-    (3584, 384, ("core", "xy", "all_z")),
-    (3968, 384, ("core", "xy", "all_z")),
+    (0, 512, ("core", "z1", "p", "q", "z2")),
+    (512, 512, ("core", "p", "q", "z")),
+    (1024, 512, ("core", "z1", "xy", "z2")),
+    (1536, 512, ("core", "p", "q", "line")),
+    (2048, 512, ("core", "p", "q", "z1", "z2")),
+    (2560, 512, ("core", "z1", "z2", "xy")),
+    (3072, 512, ("core", "p", "q", "line")),
+    (3584, 256, ("core", "p", "q", "line")),
+    (3840, 256, ("core", "p", "q", "line")),
+    (4096, 256, ("core", "xy", "line")),
     (4352, 256, ("core", "xy", "all_z")),
 )
 SCHEDULE = (
-    -1, -1, -1, 0, 1, -1, 2, -1, -1, -1, -1, 3, 4, 5, 0, -1, 10, -1, 1, 2, -1, -1, -1, 4, 3, 6, -1, 0,
-    -1, 10, -1, -1, 5, 4, 1, 7, -1, 3, -1, 0, 2, -1, 6, 5, 8, -1, 1, 10, 4, -1, 3, -1, 7, 5, 9, 0, 11,
-    2, 8, 6, 1, 5, 4, 3, 9, 12, 0, 11, 7, 5, 2, 4, 2, 8, 3, 6, 1, 0, 4, 0, 9, 4, 7, 11, 7, 8, 3, 8, 6,
-    3, 5, 9, 1, 6, 5, 9, 1,
+    -1, -1, -1, 0, -1, 2, 1, -1, -1, -1, -1, 3, 4, 5, 0, -1, 1, 11, -1, 2, -1, -1, 3, -1, 5, 4, 6, 0,
+    1, -1, 7, -1, 11, -1, -1, 4, 3, 2, -1, 6, 8, 0, 7, -1, 5, -1, -1, 4, 9, 6, 3, 1, -1, 8, 7, 10, -1,
+    13, 5, 0, 2, 12, 11, 4, 6, 3, 8, 9, 7, 10, 1, 0, 2, 4, 3, 6, 8, 7, 9, 5, 12, 1, 0, 4, 8, 6, 9, 10,
+    7, 2, 3, 1, 0, 8, 4, 5, 9, 6, 1, 7, 12, 10, 2, 3, 8, 10, 2, 4, 3, 0, 4, 9, 0, 6, 5, 7, 9, 8, 6, 5,
+    7, 8,
 )
 
 
@@ -74,7 +77,7 @@
     inputs_ref, lengths_ref, cot_ref, pool_ref,
     qkv_hbm, qb_ref, vb_ref, out_hbm, ob_ref, g1_ref, b1_ref,
     up_hbm, ub_ref, down_hbm, db_ref, g2_ref, b2_ref,
-    block_ref, pooled_ref, igrad_ref, full, small_ref,
+    block_ref, pooled_ref, igrad_ref, full, wide, small_ref,
     x, cot, qkv_w, out_w, up_w, down_w, qkv_t,
     q_t, kd_t, kz_t, v_x, probs, inv, c_t, y1, r1, first_low, active, slope,
     lower, gsum, g_low, g_up, g_hid, gc_t, gj_t, bout, igr, pool,
@@ -112,6 +115,14 @@
         "x": (xx, x_peer),
         "z1": (lax.rem(zz, 2), (flip(dp, 2), sq)),
         "z2": (lax.div(zz, 2), (flip(dp, 4), sq)),
+        "p": (
+            xx + core * (yy - xx),
+            (dp + (1 - core) * (flip(dp, 1) - dp), sq + core * (flip(sq, 2) - sq)),
+        ),
+        "q": (
+            yy + core * (xx - yy),
+            (dp + core * (flip(dp, 1) - dp), sq + (1 - core) * (flip(sq, 2) - sq)),
+        ),
     }
 
     loads = [
@@ -303,6 +314,9 @@
     groups = {name: (digit, [(peer, 1 - digit)]) for name, (digit, peer) in halvings.items()}
     groups["xy"] = (plane, plane_peers)
     groups["z"] = groups["all_z"] = (zz, z_places)
+    at_end = lax.rem(zz, 3) == 0
+    z_pair = (dp + 2 * (flip(zz, 1) - zz), sq)
+    z_across = (dp + 2 * (3 - 2 * zz), sq)
     refs = list(travel_refs)
 
     def travel(first, rows, way):
@@ -318,6 +332,53 @@
         held, offset, base, size = part, first, first, rows
         places = []
         for level, name in enumerate(way):
+            if name == "line":
+                mine, spot = held.at[piece(offset, size)], full.at[piece(base, size)]
+                got = gots[level]
+                inward, across, outward = (
+                    remote(src, dst, send.at[n], recv.at[n], peer)
+                    for n, src, dst, peer in (
+                        (next(used), mine, got.at[0], z_pair),
+                        (next(used), got.at[2], got.at[1], z_across),
+                        (next(used), spot, spot, z_pair),
+                    )
+                )
+
+                @pl.when(at_end)
+                def _():
+                    inward.start()
+
+                yield
+
+                @pl.when(at_end)
+                def _():
+                    inward.wait_send()
+
+                @pl.when(jnp.logical_not(at_end))
+                def _():
+                    inward.wait_recv()
+                    got[2] = add(mine[...], got[0])
+                    across.start()
+
+                yield
+
+                @pl.when(jnp.logical_not(at_end))
+                def _():
+                    across.wait()
+                    full[piece(base, size), :] = add(got[2], got[1])
+                    outward.start()
+
+                yield
+
+                @pl.when(at_end)
+                def _():
+                    outward.wait_recv()
+
+                @pl.when(jnp.logical_not(at_end))
+                def _():
+                    outward.wait_send()
+
+                continue
             index, peers = groups[name]
             moves = []
             if name == "all_z":
@@ -371,6 +432,9 @@
             yield
             for move in moves:
                 move.wait()
+        last = min(first + rows, WIDE)
+        if first < last:
+            wide[first:last, :] = full[first:last, :].astype(F32)
 
     def vectors(mine, got, planes, zs, more, send, recv):
         move = remote(mine, got, send.at[0], recv.at[0], core_peer)
@@ -550,14 +614,28 @@
 
 
 def finish_kernel(
-    grads_ref, small_ref, pool_ref, bl_ref, ig_ref,
+    grads_ref, wide_ref, small_ref, pool_ref, bl_ref, ig_ref,
     block_ref, pooled_ref, igrad_ref, qkv_ref, qb_ref, vb_ref, out_ref, ob_ref, g1_ref, b1_ref,
     up_ref, ub_ref, down_ref, db_ref, g2_ref, b2_ref,
-    wide, out_sem, sem,
+    qkv_wide, sem,
 ):
+    copies = [(wide_ref.at[pl.ds(0, FF)], down_ref)]
+    copies += [
+        (wide_ref.at[pl.ds(FF + i * D, D)], up_ref.at[:, pl.ds(i * D, D)]) for i in range(4)
+    ]
+    copies += [(wide_ref.at[pl.ds(2 * FF, D)], out_ref), (bl_ref, block_ref), (ig_ref, igrad_ref)]
     moves = []
-    for i, (src, dst) in enumerate(((bl_ref, block_ref), (ig_ref, igrad_ref))):
+    for i, (src, dst) in enumerate(copies):
         move = pltpu.make_async_copy(src, dst, sem.at[i])
+        move.start()
+        moves.append(move)
+    for i in range(3):
+        first = WIDE + i * 64
+        turned = [grads_ref[first + g * 192 : first + g * 192 + 64, :] for g in range(H // 2)]
+        qkv_wide[i] = jnp.concatenate(turned, axis=0).T.astype(F32)
+        move = pltpu.make_async_copy(
+            qkv_wide.at[i], qkv_ref.at[:, pl.ds(i * D, D)], sem.at[len(copies) + i]
+        )
         move.start()
         moves.append(move)
     for i in range(4):
@@ -566,26 +644,6 @@
         pooled_ref[m] = pool_ref[m, :1, :]
     for row, ref in ((4, db_ref), (5, ob_ref), (6, qb_ref), (7, vb_ref), (8, g1_ref), (9, b1_ref), (10, g2_ref), (11, b2_ref)):
         ref[...] = small_ref[row, :]
-    for i in range(12):
-        if i < 9:
-            wide[i] = grads_ref[i * D : (i + 1) * D, :].astype(F32)
-        else:
-            first = 9 * D + (i - 9) * 64
-            turned = [grads_ref[first + g * 192 : first + g * 192 + 64, :] for g in range(H // 2)]
-            wide[i] = jnp.concatenate(turned, axis=0).T.astype(F32)
-        span = pl.ds((i % 4) * D, D)
-        if i < 4:
-            copies = [(wide.at[i], down_ref.at[span])]
-        elif i < 8:
-            copies = [(wide.at[i], up_ref.at[:, span])]
-        elif i == 8:
-            copies = [(wide.at[i], out_ref)]
-        else:
-            copies = [(wide.at[i], qkv_ref.at[:, pl.ds((i - 9) * D, D)])]
-        for j, (src, dst) in enumerate(copies):
-            move = pltpu.make_async_copy(src, dst, out_sem.at[i, j])
-            move.start()
-            moves.append(move)
     for move in moves:
         move.wait()
 
@@ -594,7 +652,10 @@
     gots, sums, count = [], [], extra
     for name in way:
         peers = {"xy": 3, "z": 3, "all_z": 3}.get(name, 1)
-        if name == "all_z":
+        if name == "line":
+            gots.append(pltpu.VMEM((3, rows, D), BF16))
+            count += 3
+        elif name == "all_z":
             gots.append(pltpu.VMEM((4, rows, D), BF16))
             count += 3
         else:
@@ -642,10 +703,10 @@
     results = pl.pallas_call(
         functools.partial(kernel, ndp),
         out_shape=(
-            v(*inputs.shape), v(4, 8, D, dtype=F32), v(*inputs.shape), v(CHUNKS * ROWS, D), v(16, D, dtype=F32),
+            v(*inputs.shape), v(4, 8, D, dtype=F32), v(*inputs.shape), v(CHUNKS * ROWS, D), v(WIDE, D, dtype=F32), v(16, D, dtype=F32),
         ),
         in_specs=in_specs,
-        out_specs=(vmem,) * 5,
+        out_specs=(vmem,) * 6,
         scratch_shapes=[
             v(512, D), v(512, D), v(D, 3 * D), v(D, D), v(D, FF), v(FF, D), v(3 * D, D),
             v(D, 512), v(D, 512), v(D, 512), v(H * VROWS, 512), v(H, 512, 512), v(H, 8, 512, dtype=F32),
@@ -660,10 +721,10 @@
             *[item for rows in (16, 8) for item in vector_scratch(rows, extra)],
         ],
         compiler_params=pltpu.CompilerParams(
-            collective_id=0, has_side_effects=True, vmem_limit_bytes=56 * 2**20
+            collective_id=0, has_side_effects=True, vmem_limit_bytes=52 * 2**20
         ),
     )(*args)
-    block, pooled, igrad, grads, small = results
+    block, pooled, igrad, grads, wide, small = results
 
     def shape(*dims, dtype=F32):
         return jax.ShapeDtypeStruct(dims, dtype)
@@ -675,14 +736,14 @@
             shape(D, 3 * D), shape(D), shape(D), shape(D, D), shape(D), shape(D), shape(D),
             shape(D, FF), shape(FF), shape(FF, D), shape(D), shape(D), shape(D),
         ),
-        in_specs=[vmem] * 5,
+        in_specs=[vmem] * 6,
         out_specs=(
             any_spec, vmem, any_spec, any_spec, vmem, vmem, any_spec, vmem, vmem, vmem,
             any_spec, vmem, any_spec, vmem, vmem, vmem,
         ),
-        scratch_shapes=[v(12, D, D, dtype=F32), dma((12, 3)), dma((2,))],
-        compiler_params=pltpu.CompilerParams(vmem_limit_bytes=24 * 2**20),
-    )(grads, small, pooled, block, igrad)
+        scratch_shapes=[v(3, D, D, dtype=F32), dma((11,))],
+        compiler_params=pltpu.CompilerParams(vmem_limit_bytes=8 * 2**20),
+    )(grads, wide, small, pooled, block, igrad)
     return outs
 
 

time: 74.2 us -> 71.6 us (0.965)
  Pallas kernels: 73.2 us -> 70.6 us
    pallas_call x1, Pallas kernels: 69 us -> 66.7 us  [body(): pl.pallas_call(functools.partial(kernel, ndp), out_shape=(v(*inputs.shape...]
where the time goes in v5:
time: 71.6 us; the launch traced here: 71.5 us
  Pallas kernels  70.6 us (99%)
  between operations  0.84 us (1%)
    pallas_call x1, Pallas kernels, body(): pl.pallas_call(functools.partial(kernel, ndp), out_shape=(v(*inputs.shape...  66.7 us
    pallas_call x1, Pallas kernels, body(): pl.pallas_call(finish_kernel, out_shape=(shape(*inputs.shape, dtype=BF16)...  3.92 us

profile of v5, /device:TPU:0, one launch (start us, length us, event | category | flops | bytes accessed | tf_op | source)
XLA Modules:
  0.0 71.5 jit_solution(14748893984839451014)
XLA Ops:
  0.7 66.7 %shard_map.288 = (bf16[4,1,128,384]{3,2,1,0:T(8,128)(2,1)S(1)}, f32[4,8,384]{2,1,0:T(8,128)S(1)}, bf16[4,1,128,384]{3,2,1,0:T(8,128)(2,1)S(1)}, bf16[4608,384]{1...) custom-call(bf16[4,1,128,384]{3,2,1,0:T(8,128)(2,1)} %inputs_ref.1, s32[1,4]{1,0:T(1,128)} %bitcast.3, ...), custom_call_target="tpu_custom_call" | custom-call | tf_op jit(solution)/shard_map/pallas_call | solution.py:703
  67.4 3.9 %shard_map.289 = (bf16[4,1,128,384]{3,2,1,0:T(8,128)(2,1)}, f32[4,1,384]{2,1,0:T(1,128)}, bf16[4,1,128,384]{3,2,1,0:T(8,128)(2,1)}, f32[384,1152]{1,0:T(8,128)},...) custom-call(bf16[4608,384]{1,0:T(8,128)(2,1)S(1)} %get-tuple-element, ...), custom_call_target="tpu_custom_call" | custom-call | tf_op jit(solution)/shard_map/pallas_call | solution.py:732

commit v6 on v5

--- a/solution.py
+++ b/solution.py
@@ -81,7 +81,7 @@
     x, cot, qkv_w, out_w, up_w, down_w, qkv_t,
     q_t, kd_t, kz_t, v_x, probs, inv, c_t, y1, r1, first_low, active, slope,
     lower, gsum, g_low, g_up, g_hid, gc_t, gj_t, bout, igr, pool,
-    part, small, late, up_row,
+    part, small, late, up_row, vecs, up_vec, pool_in, vec_sem,
     w_sem, loc_sem, in_send, in_recv, out_send, out_recv, pool_send, pool_recv,
     s_a, s_b, gs_t, gs_n, p_n, *travel_refs,
 ):
@@ -125,6 +125,9 @@
         ),
     }
 
+    barrier = pltpu.get_barrier_semaphore()
+    for peer in greeted:
+        pl.semaphore_signal(barrier, inc=1, device_id=peer, device_id_type=MESH)
     loads = [
         pltpu.make_async_copy(src, dst, w_sem.at[i])
         for i, (src, dst) in enumerate(
@@ -137,11 +140,14 @@
     own_x = pltpu.make_async_copy(inputs_ref.at[sq, 0], x.at[own_rows], loc_sem.at[0])
     own_c = pltpu.make_async_copy(cot_ref.at[sq, 0], cot.at[own_rows], loc_sem.at[1])
     own_x.start()
+    vec_refs = (qb_ref, vb_ref, ob_ref, g1_ref, b1_ref, db_ref, g2_ref, b2_ref)
+    vec_moves = [pltpu.make_async_copy(src, dst, vec_sem.at[i]) for i, (src, dst) in enumerate(zip(vec_refs, vecs))]
+    vec_moves.append(pltpu.make_async_copy(ub_ref, up_vec, vec_sem.at[8]))
+    vec_moves.append(pltpu.make_async_copy(pool_ref, pool_in, vec_sem.at[9]))
+    for move in vec_moves:
+        move.start()
     own_c.start()
 
-    barrier = pltpu.get_barrier_semaphore()
-    for peer in greeted:
-        pl.semaphore_signal(barrier, inc=1, device_id=peer, device_id_type=MESH)
     pl.semaphore_wait(barrier, len(greeted))
 
     def remote(src, dst, send, recv, peer):
@@ -162,14 +168,14 @@
         move.start()
 
     span = lengths_ref[0, sq]
-    query_bias, value_bias, out_bias, gain_one, bias_one, up_bias, down_bias, gain_two, bias_two = (
-        ref[...].reshape(1, -1)
-        for ref in (qb_ref, vb_ref, ob_ref, g1_ref, b1_ref, ub_ref, db_ref, g2_ref, b2_ref)
-    )
-    up_row[...] = up_bias
     count = span.astype(F32)
     lane_valid = lax.broadcasted_iota(jnp.int32, (1, 512), 1) < span
-
+    for move in vec_moves:
+        move.wait()
+    query_bias, value_bias, out_bias, gain_one, bias_one, down_bias, gain_two, bias_two = (
+        vec[...].reshape(1, -1) for vec in vecs
+    )
+    up_row[...] = up_vec[...].reshape(1, -1)
     loads[0].wait()
 
     for i in range(3):
@@ -255,7 +261,7 @@
     for move in c_moves:
         move.wait()
     chosen = lax.broadcasted_iota(jnp.int32, (4, D), 0) == sq
-    pool_share = jnp.sum(jnp.where(chosen, pool_ref[0].astype(F32), 0.0), axis=0, keepdims=True) / count
+    pool_share = jnp.sum(jnp.where(chosen, pool_in[0].astype(F32), 0.0), axis=0, keepdims=True) / count
 
     zero_row = jnp.zeros((1, D), F32)
 
@@ -617,14 +623,27 @@
     grads_ref, wide_ref, small_ref, pool_ref, bl_ref, ig_ref,
     block_ref, pooled_ref, igrad_ref, qkv_ref, qb_ref, vb_ref, out_ref, ob_ref, g1_ref, b1_ref,
     up_ref, ub_ref, down_ref, db_ref, g2_ref, b2_ref,
-    qkv_wide, sem,
+    qkv_wide, rows_1d, row_ub, row_pool, sem,
 ):
+    moves = []
+    for i in range(4):
+        row_ub[i * D : (i + 1) * D] = small_ref[i, :]
+    for m in range(4):
+        row_pool[m] = pool_ref[m, :1, :]
+    for i, (row, ref) in enumerate(
+        ((4, db_ref), (5, ob_ref), (6, qb_ref), (7, vb_ref), (8, g1_ref), (9, b1_ref), (10, g2_ref), (11, b2_ref))
+    ):
+        rows_1d[i][...] = small_ref[row, :]
+        moves.append(pltpu.make_async_copy(rows_1d[i], ref, sem.at[11 + i]))
+    moves.append(pltpu.make_async_copy(row_ub, ub_ref, sem.at[19]))
+    moves.append(pltpu.make_async_copy(row_pool, pooled_ref, sem.at[20]))
+    for move in moves:
+        move.start()
     copies = [(wide_ref.at[pl.ds(0, FF)], down_ref)]
     copies += [
         (wide_ref.at[pl.ds(FF + i * D, D)], up_ref.at[:, pl.ds(i * D, D)]) for i in range(4)
     ]
     copies += [(wide_ref.at[pl.ds(2 * FF, D)], out_ref), (bl_ref, block_ref), (ig_ref, igrad_ref)]
-    moves = []
     for i, (src, dst) in enumerate(copies):
         move = pltpu.make_async_copy(src, dst, sem.at[i])
         move.start()
@@ -638,12 +657,6 @@
         )
         move.start()
         moves.append(move)
-    for i in range(4):
-        ub_ref[i * D : (i + 1) * D] = small_ref[i, :]
-    for m in range(4):
-        pooled_ref[m] = pool_ref[m, :1, :]
-    for row, ref in ((4, db_ref), (5, ob_ref), (6, qb_ref), (7, vb_ref), (8, g1_ref), (9, b1_ref), (10, g2_ref), (11, b2_ref)):
-        ref[...] = small_ref[row, :]
     for move in moves:
         move.wait()
 
@@ -695,11 +708,8 @@
         norm2_gain, norm2_bias,
     )
     in_specs = [
-        any_spec, smem, any_spec, vmem,
-        any_spec, vmem, vmem, any_spec, vmem,
-        vmem, vmem, any_spec, vmem, any_spec, vmem,
-        vmem, vmem,
-    ]
+        any_spec, smem,
+    ] + [any_spec] * 15
     results = pl.pallas_call(
         functools.partial(kernel, ndp),
         out_shape=(
@@ -715,6 +725,7 @@
             v(D, 512), v(3 * D, 512), v(512, D), v(512, D), v(4, 8, D, dtype=F32),
             v(CHUNKS * ROWS, D),
             v(16, D, dtype=F32), v(8, D, dtype=F32), v(1, FF, dtype=F32),
+            [v(D, dtype=F32)] * 8, v(FF, dtype=F32), v(1, 4, D), dma((10,)),
             dma((4,)), dma((4,)), dma((2, 3)), dma((2, 3)), dma((2, 3)), dma((2, 3)), dma((3,)), dma((3,)),
             v(512, 512, dtype=F32), v(512, 512, dtype=F32), v(512, 512), v(512, 512), v(512, 512),
             *[item for _, rows, way in PLAN for item in travel_scratch(rows, way, extra)],
@@ -737,11 +748,10 @@
             shape(D, FF), shape(FF), shape(FF, D), shape(D), shape(D), shape(D),
         ),
         in_specs=[vmem] * 6,
-        out_specs=(
-            any_spec, vmem, any_spec, any_spec, vmem, vmem, any_spec, vmem, vmem, vmem,
-            any_spec, vmem, any_spec, vmem, vmem, vmem,
-        ),
-        scratch_shapes=[v(3, D, D, dtype=F32), dma((11,))],
+        out_specs=(any_spec,) * 16,
+        scratch_shapes=[
+            v(3, D, D, dtype=F32), [v(D, dtype=F32)] * 8, v(FF, dtype=F32), v(4, 1, D, dtype=F32), dma((21,)),
+        ],
         compiler_params=pltpu.CompilerParams(vmem_limit_bytes=8 * 2**20),
     )(grads, wide, small, pooled, block, igrad)
     return outs

time: 71.6 us -> 71 us (level)
  no operation moved by 1% of the time
where the time goes in v6:
time: 71 us; the launch traced here: 70.9 us
  Pallas kernels  70 us (99%)
  between operations  0.84 us (1%)
    pallas_call x1, Pallas kernels, body(): pl.pallas_call(functools.partial(kernel, ndp), out_shape=(v(*inputs.shape...  66.6 us
    pallas_call x1, Pallas kernels, body(): pl.pallas_call(finish_kernel, out_shape=(shape(*inputs.shape, dtype=BF16)...  3.4 us

profile of v6, /device:TPU:0, one launch (start us, length us, event | category | flops | bytes accessed | tf_op | source)
XLA Modules:
  0.0 70.9 jit_solution(10796740624549716150)
XLA Ops:
  0.7 66.6 %shard_map.288 = (bf16[4,1,128,384]{3,2,1,0:T(8,128)(2,1)S(1)}, f32[4,8,384]{2,1,0:T(8,128)S(1)}, bf16[4,1,128,384]{3,2,1,0:T(8,128)(2,1)S(1)}, bf16[4608,384]{1...) custom-call(bf16[4,1,128,384]{3,2,1,0:T(8,128)(2,1)} %inputs_ref.1, s32[1,4]{1,0:T(1,128)} %bitcast.3, ...), custom_call_target="tpu_custom_call" | custom-call | tf_op jit(solution)/shard_map/pallas_call | solution.py:713
  67.3 3.4 %shard_map.289 = (bf16[4,1,128,384]{3,2,1,0:T(8,128)(2,1)}, f32[4,1,384]{2,1,0:T(1,128)}, bf16[4,1,128,384]{3,2,1,0:T(8,128)(2,1)}, f32[384,1152]{1,0:T(8,128)},...) custom-call(bf16[4608,384]{1,0:T(8,128)(2,1)S(1)} %get-tuple-element, ...), custom_call_target="tpu_custom_call" | custom-call | tf_op jit(solution)/shard_map/pallas_call | solution.py:743
